TPU v7x, 256 devices: a whole 4x4x8 slice. The times are simulated.
256 devices in a mesh: grp: 2 (over x_lo), lat: 16 (over z, x_hi), lon: 8 (over y, core).
Axes of the slice: x: 4 (x_hi: 2, x_lo: 2; x = x_hi * 2 + x_lo), y: 4, z: 8, core: 2. Of those that a mesh axis runs over, the one named last changes fastest.
Arguments:
- coupled_state: bfloat16 [2, 80, 256, 1024], P('grp', None, 'lat', 'lon'), may hold values from -6 to 6
- land_mask: int32 [256, 1024], P('lat', 'lon'), may hold values 0 or 1
- regrid_offsets: int32 [2, 2, 4, 256, 1024], P('grp', None, None, 'lat', 'lon'), may hold values from -8 to 8
- regrid_weights: float32 [2, 4, 256, 1024], P('grp', None, 'lat', 'lon'), may hold values from 0.1 to 0.4
- surface_proj: float32 [2, 4, 80], replicated, may hold values from -0.625 to 0.625
- atm_in: bfloat16 [384, 84], replicated, may hold values from -0.625 to 0.625
- atm_bias: float32 [384], replicated, may hold values from -3 to 3
- atm_out: bfloat16 [80, 384], replicated, may hold values from -0.3125 to 0.3125
- ocn_in: bfloat16 [200, 9, 84], replicated, may hold values from -0.21875 to 0.21875
- ocn_bias: float32 [200], replicated, may hold values from -3 to 3
- ocn_out: bfloat16 [80, 9, 200], replicated, may hold values from -0.125 to 0.125
Outputs:
- next_state: bfloat16 [2, 80, 256, 1024], P('grp', None, 'lat', 'lon')
All inputs are finite; a program needn't handle non-finite values. No bound on the sum of `land_mask` on one device may be relied on, other than what follows from the above.
Results may differ from a plain program's by a relative error of at most 0.008.
Values may be sent and summed in bfloat16 or wider, within the bound.
A program may use at most 64 MiB of HBM per device.

v0:
```python
import functools

import jax
import jax.numpy as jnp
from jax import lax
from jax.experimental import pallas as pl
from jax.experimental.pallas import tpu as pltpu
from jax.sharding import PartitionSpec as P

BF = jnp.bfloat16
F32 = jnp.float32
I32 = jnp.int32
MESH = pl.DeviceIdType.MESH

STEPS = 2
HW = 8
CH = 80
HO = 200
HOP = 208
ROWS = 16
LANES = 128
TALL = ROWS + 4


def iota(shape, axis):
    return lax.broadcasted_iota(I32, shape, axis)


def one_hot(shape, test):
    return jnp.where(test, 1.0, 0.0).astype(F32).astype(BF)


def gelu(x):
    inner = x * (0.7978845608028654 + 0.035677408136300125 * (x * x))
    half = 0.5 * x
    return half + half * jnp.tanh(inner)


def thirds(x):
    high = x.astype(BF).astype(F32)
    middle = (x - high).astype(BF).astype(F32)
    return high, middle, x - high - middle


def bias_columns(bias, rows):
    count = bias.shape[0]
    spread = jnp.broadcast_to(bias.reshape(1, count), (rows, count))
    same = iota((rows, count), 0) == iota((rows, count), 1)
    return thirds(jnp.sum(jnp.where(same, spread, 0.0), axis=1, keepdims=True))


def kernel(
    lats,
    lons,
    state_ref,
    mask_ref,
    offsets_ref,
    weights_ref,
    proj_ref,
    atm_in_ref,
    atm_bias_ref,
    atm_out_ref,
    ocn_in_hbm,
    ocn_bias_ref,
    ocn_out_hbm,
    out_ref,
    flip,
    xr,
    eg,
    eg_recv,
    cp,
    cp_recv,
    sm,
    sb,
    sp,
    sp_recv,
    q,
    qe,
    qe_recv,
    gi,
    gd,
    gw,
    sd,
    fr,
    x3,
    x3e,
    w1,
    w2,
    wa,
    hid,
    he,
    hh,
    ze,
    keep,
    wet,
    pp,
    ocn_in_v,
    ocn_out_v,
    wt1,
    wt2,
    load_sem,
    s_send,
    s_recv,
    x_send,
    x_recv,
    q_send,
    q_recv,
):
    g = lax.axis_index("grp")
    i = lax.axis_index("lat")
    j = lax.axis_index("lon")
    ocean = g == 1
    air = g == 0
    has = {-1: i > 0, 0: None, 1: i < lats - 1}

    def place(group, di, dj):
        return (group, i + di, lax.rem(j + dj + lons, lons))

    def when(condition, action):
        if condition is None:
            action()
        else:
            pl.when(condition)(action)

    lane8 = iota((8, LANES), 1)
    sub8 = iota((8, LANES), 0)
    low = sub8 < 4
    lane80 = iota((CH, LANES), 1)
    lane16 = iota((16, LANES), 1)

    loads = [
        pltpu.make_async_copy(ocn_in_hbm, ocn_in_v, load_sem.at[0]),
        pltpu.make_async_copy(ocn_out_hbm, ocn_out_v, load_sem.at[1]),
    ]

    @pl.when(ocean)
    def _():
        for load in loads:
            load.start()

    for di, block, rows in ((-1, 0, slice(0, 2)), (1, 2, slice(18, 20))):
        def blank(block=block, rows=rows):
            for s in range(STEPS):
                xr[s, rows] = jnp.zeros((2, CH, LANES), BF)
                sb[s, slice(0, 48) if block == 0 else slice(112, 160)] = jnp.zeros((48, LANES), BF)
                sp_recv[s, block] = jnp.zeros((2, 16, LANES), BF)
                cp_recv[s, block // 2] = jnp.zeros((2, 16, LANES), BF)
            q[rows] = jnp.zeros((2, 8, LANES), F32)
            qe_recv[block] = jnp.zeros((2, 8, LANES), F32)

        pl.when(jnp.logical_not(has[di]))(blank)

    barrier = pltpu.get_barrier_semaphore()

    def greet(group, di, dj):
        when(
            has[di],
            lambda: pl.semaphore_signal(
                barrier, inc=1, device_id=place(group, di, dj), device_id_type=MESH
            ),
        )

    for di in (-1, 0, 1):
        for dj in (-1, 0, 1):
            greet(1 - g, di, dj)

    @pl.when(ocean)
    def _():
        for di in (-1, 0, 1):
            for dj in (-1, 0, 1):
                if di or dj:
                    greet(1, di, dj)

    def remote(src, dst, send, recv, target):
        return pltpu.make_async_remote_copy(
            src_ref=src,
            dst_ref=dst,
            send_sem=send,
            recv_sem=recv,
            device_id=target,
            device_id_type=MESH,
        )

    def s_copy(s, di, dj):
        n = 1 - di
        if dj == 0:
            src = {0: sm.at[s], 1: sm.at[s, pl.ds(16, 48)], -1: sm.at[s, pl.ds(0, 48)]}[di]
            dst = sb.at[s, pl.ds(48, 64)] if di == 0 else sb.at[s, pl.ds(0 if di == 1 else 112, 48)]
        else:
            src = sp.at[s]
            dst = sp_recv.at[s, n, 0 if dj == 1 else 1]
        return remote(src, dst, s_send.at[s, n, dj + 1], s_recv.at[s, n, dj + 1], place(1 - g, di, dj))

    def x_copy(s, di, dj):
        n = 1 - di
        if dj == 0:
            src = xr.at[s, pl.ds(16 if di == 1 else 2, 2)]
            dst = xr.at[s, pl.ds(0 if di == 1 else 18, 2)]
        elif di == 0:
            src = eg.at[s]
            dst = eg_recv.at[s, 0 if dj == 1 else 1]
        else:
            src = cp.at[s]
            dst = cp_recv.at[s, n // 2, 0 if dj == 1 else 1]
        return remote(src, dst, x_send.at[s, n, dj + 1], x_recv.at[s, n, dj + 1], place(1, di, dj))

    def q_copy(di, dj):
        n = 1 - di
        if dj == 0:
            src = q.at[pl.ds(16 if di == 1 else 2, 2)]
            dst = q.at[pl.ds(0 if di == 1 else 18, 2)]
        else:
            src = qe
            dst = qe_recv.at[n, 0 if dj == 1 else 1]
        return remote(src, dst, q_send.at[n, dj + 1], q_recv.at[n, dj + 1], place(1, di, dj))

    around = [(di, dj) for di in (-1, 0, 1) for dj in (-1, 0, 1)]
    ring = [(di, dj) for di, dj in around if di or dj]

    def start_all(make, pairs):
        for di, dj in pairs:
            when(has[di], lambda di=di, dj=dj: make(di, dj).start())

    def wait_arrivals(make, pairs):
        for di, dj in pairs:
            when(has[-di], lambda di=di, dj=dj: make(di, dj).wait_recv())

    def wait_departures(make, pairs):
        for di, dj in pairs:
            when(has[di], lambda di=di, dj=dj: make(di, dj).wait_send())

    flip[...] = state_ref[0].astype(F32).reshape(CH * ROWS, LANES)

    def to_rows(r, c):
        xr[0, r + 2] = flip[pl.ds(r, CH, stride=ROWS), :].astype(BF)
        return c

    lax.fori_loop(0, ROWS, to_rows, 0, unroll=4)

    wet_values = mask_ref[...].astype(F32)
    wet[...] = wet_values
    kept = jnp.where(ocean, wet_values, 1.0)
    for pair in range(ROWS // 2):
        upper = jnp.broadcast_to(kept[2 * pair : 2 * pair + 1], (8, LANES))
        lower = jnp.broadcast_to(kept[2 * pair + 1 : 2 * pair + 2], (8, LANES))
        keep[8 * pair : 8 * pair + 8] = jnp.where(low, upper, lower)
    high, middle, rest = thirds(proj_ref[g])
    pp[...] = jnp.concatenate([high, high, middle, middle, rest, rest], 0).astype(BF)

    def surface(s):
        def four(m, c):
            t = 4 * m + 2
            rows = jnp.concatenate([xr[s, t + u] for u in range(4)], 1)
            parts = jnp.dot(pp[...], rows, preferred_element_type=F32)
            fields = parts[0:8] + parts[8:16] + parts[16:24]
            pairs = [
                jnp.where(
                    low,
                    fields[:, 256 * u : 256 * u + 128],
                    fields[:, 256 * u + 128 : 256 * u + 256],
                )
                for u in range(2)
            ]
            start = pl.multiple_of(16 * m, 16)
            both = jnp.concatenate(pairs, 0) * keep[pl.ds(start, 16), :]
            sm[s, pl.ds(start, 16), :] = both.astype(BF)
            return c

        lax.fori_loop(0, 4, four, 0, unroll=True)
        packed = jnp.zeros((16, LANES), F32)
        slot = ((lane16 + 16) >> 5) & 3
        for m in range(4):
            tile = sm[s, 16 * m : 16 * m + 16].astype(F32)
            packed = jnp.where(slot == m, pltpu.roll(tile, 32 * m, 1) if m else tile, packed)
        sp[s] = packed.astype(BF)

    def edges(s):
        def add(t, acc):
            return jnp.where((lane80 >> 2) == t, pltpu.roll(xr[s, t], 4 * t + 2, 1), acc)

        own = lax.fori_loop(2, 18, add, jnp.zeros((CH, LANES), BF), unroll=4)
        eg[s] = own
        packed = jnp.zeros((16, LANES), BF)
        for part in range(5):
            tile = pltpu.roll(own[16 * part : 16 * part + 16], 64 + 8 * part, 1)
            place_of = lane16 - 8 * part
            inside = ((place_of >= 0) & (place_of < 8)) | ((place_of >= 72) & (place_of < 80))
            packed = jnp.where(inside, tile, packed)
        cp[s] = packed

    surface(0)

    for k in range(4):
        code = (offsets_ref[0, 0, k] + HW) * 32 + (offsets_ref[0, 1, k] + HW)
        flip[16 * k : 16 * k + 16] = code.astype(F32)
        flip[64 + 16 * k : 64 + 16 * k + 16] = weights_ref[0, k]
    for r in range(ROWS):
        q[r + 2] = flip[pl.ds(r, 8, stride=ROWS), :]

    @pl.when(ocean)
    def _():
        edges(0)

        def add(t, acc):
            return jnp.where((lane8 >> 2) == t, pltpu.roll(q[t], 4 * t + 2, 1), acc)

        qe[...] = lax.fori_loop(2, 18, add, jnp.zeros((8, LANES), F32))

    neighbours = 1 + has[-1].astype(I32) + has[1].astype(I32)
    pl.semaphore_wait(barrier, 3 * neighbours + g * (3 * neighbours - 1))

    start_all(functools.partial(s_copy, 0), around)

    @pl.when(ocean)
    def _():
        start_all(functools.partial(x_copy, 0), ring)
        start_all(q_copy, ring)

    @pl.when(ocean)
    def _():
        for load in loads:
            load.wait()

        def widen1(o, c):
            wt1[pl.ds(pl.multiple_of(16 * o, 16), 9), 0:84] = ocn_in_v[o].astype(F32)
            return c

        lax.fori_loop(0, HO, widen1, 0, unroll=8)
        wt1[16 * HO :, :] = jnp.zeros((16 * (HOP - HO), LANES), F32)
        wt2[1] = jnp.zeros((16 * CH, LANES), F32)

        def widen2(o, c):
            taps = ocn_out_v[o].astype(F32)
            wt2[0, pl.ds(pl.multiple_of(16 * o, 16), 9), :] = taps[:, 0:128]
            wt2[1, pl.ds(pl.multiple_of(16 * o, 16), 9), 0 : HO - 128] = taps[:, 128:HO]
            return c

        lax.fori_loop(0, CH, widen2, 0, unroll=8)
        channel = iota((84, 256), 0)
        lane = iota((84, 256), 1)
        bias = bias_columns(ocn_bias_ref[...], HOP)
        lane_w = iota((HOP, 256), 1)
        for a in range(3):
            total = jnp.zeros((HOP, 256), F32)
            for b in range(3):
                target = jnp.where(channel < CH, channel + CH * b, channel + 240 + 4 * b - CH)
                total = total + jnp.dot(
                    wt1[pl.ds(3 * a + b, HOP, stride=16), 0:84].astype(BF),
                    one_hot((84, 256), lane == target),
                    preferred_element_type=F32,
                )
            if a == 1:
                for part in range(3):
                    total = jnp.where(lane_w == 252 + part, bias[part], total)
            w1[a] = total.astype(BF)
            for b in range(3):
                rows = pl.ds(3 * a + b, CH, stride=16)
                halves = [wt2[half, rows, :].astype(BF) for half in range(2)]
                w2[a, CH * b : CH * b + CH, :] = jnp.concatenate(halves, 1)[:, 0:HOP]

    @pl.when(air)
    def _():
        total = jnp.dot(
            atm_in_ref[...],
            one_hot((84, 96), iota((84, 96), 0) == iota((84, 96), 1)),
            preferred_element_type=F32,
        )
        bias = bias_columns(atm_bias_ref[...], 384)
        lane = iota((384, 96), 1)
        for part in range(3):
            total = jnp.where(lane == 84 + part, bias[part], total)
        wa[...] = total.astype(BF)

    def decode(values, t, column, row):
        for kp in range(2):
            def spread(base):
                first = jnp.broadcast_to(values[base + 2 * kp : base + 2 * kp + 1], (8, LANES))
                second = jnp.broadcast_to(values[base + 2 * kp + 1 : base + 2 * kp + 2], (8, LANES))
                return jnp.where(low, first, second)

            code = spread(0).astype(I32)
            source = column + (code & 31) - HW
            inside = (source >= 0) & (source < LANES)
            gi[t, kp] = (source & (LANES - 1)) + jnp.where(inside, 0, LANES)
            gd[t, kp] = (code >> 5) + row
            gw[t, kp] = spread(4)

    def decode_row(t, c):
        decode(q[t], t, lane8, 0)
        return c

    lax.fori_loop(2, 18, decode_row, 0, unroll=2)

    @pl.when(ocean)
    def _():
        wait_arrivals(q_copy, ring)
        lax.fori_loop(0, 2, decode_row, 0)
        lax.fori_loop(18, 20, decode_row, 0)
        pos = lane8 & 3
        beside = [jnp.where(pos < 2, qe_recv[n, 0], qe_recv[n, 1]) for n in range(3)]
        ends = jnp.where(
            lane8 < 64, pltpu.roll(beside[0], 64, 1), pltpu.roll(beside[2], 64, 1)
        )
        values = jnp.where((lane8 >= 8) & (lane8 < 72), beside[1], ends)
        decode(values, TALL, jnp.where(pos < 2, pos - 2, pos + 126), lane8 >> 2)

    def spread_pair(row, which, values):
        turned = pltpu.roll(values, 4, 0)
        sd[row, which] = jnp.where(low, values, turned)
        sd[row + 1, which] = jnp.where(low, turned, values)

    def sources(s):
        def main(m, c):
            tile = sb[s, pl.ds(pl.multiple_of(16 * m, 16), 16), :].astype(F32)
            spread_pair(4 * m, 0, tile[0:8])
            spread_pair(4 * m + 2, 0, tile[8:16])
            return c

        lax.fori_loop(0, 10, main, 0, unroll=2)
        right = ((lane16 + 16) & 31) >= 16
        for n in range(3):
            tile = jnp.where(right, sp_recv[s, n, 1].astype(F32), sp_recv[s, n, 0].astype(F32))
            for m in range(4):
                row = 16 * n + 4 * m - 4
                if 0 <= row < 40:
                    turned = pltpu.roll(tile, LANES - 32 * m, 1) if m else tile
                    spread_pair(row, 1, turned[0:8])
                    spread_pair(row + 2, 1, turned[8:16])

    def take(values, index):
        return jnp.take_along_axis(values, index, axis=1, mode="promise_in_bounds")

    def combine(t, picked):
        total = picked[0] * gw[t, 0] + picked[1] * gw[t, 1]
        return total + pltpu.roll(total, 4, 0)

    def regrid_row(t, c):
        index = [gi[t, kp] & (LANES - 1) for kp in range(2)]
        beyond = [gi[t, kp] >= LANES for kp in range(2)]
        depth = [gd[t, kp] for kp in range(2)]
        picked = [jnp.zeros((8, LANES), F32) for kp in range(2)]
        for d in range(2 * HW + 1):
            here = sd[t + d + 2, 0]
            there = sd[t + d + 2, 1]
            for kp in range(2):
                value = jnp.where(beyond[kp], take(there, index[kp]), take(here, index[kp]))
                picked[kp] = jnp.where(depth[kp] == d, value, picked[kp])
        fr[t] = combine(t, picked)
        return c

    def regrid_edges():
        index = [gi[TALL, kp] & (LANES - 1) for kp in range(2)]
        beyond = [gi[TALL, kp] >= LANES for kp in range(2)]
        depth = [gd[TALL, kp] for kp in range(2)]

        def body(d, picked):
            here = sd[d + 2, 0]
            there = sd[d + 2, 1]
            out = []
            for kp in range(2):
                value = jnp.where(beyond[kp], take(there, index[kp]), take(here, index[kp]))
                out.append(jnp.where(depth[kp] == d, value, picked[kp]))
            return tuple(out)

        zero = jnp.zeros((8, LANES), F32)
        fr[TALL] = combine(TALL, lax.fori_loop(0, TALL + 2 * HW, body, (zero, zero), unroll=4))

    def finish_row(s, r, values):
        if s + 1 < STEPS:
            xr[s + 1, r + 2] = values.astype(BF)
        else:
            flip[pl.ds(r, CH, stride=ROWS), :] = values

    def air_step(s):
        lax.fori_loop(2, 18, regrid_row, 0)
        ones = jnp.where(sub8 < 7, 1.0, 0.0)
        blank = jnp.zeros((8, LANES), F32)

        def pair(p, c):
            t = 2 * p + 2
            columns = []
            for u in range(2):
                tail = jnp.concatenate([jnp.where(low, fr[t + u], ones), blank], 0).astype(BF)
                columns.append(jnp.concatenate([xr[s, t + u], tail], 0))
            hidden = gelu(
                jnp.dot(wa[...], jnp.concatenate(columns, 1), preferred_element_type=F32)
            ).astype(BF)
            update = jnp.dot(atm_out_ref[...], hidden, preferred_element_type=F32)
            for u in range(2):
                new = xr[s, t + u].astype(F32) + update[:, 128 * u : 128 * u + 128]
                finish_row(s, 2 * p + u, new)
            return c

        lax.fori_loop(0, ROWS // 2, pair, 0)

    def ocean_step(s):
        lax.fori_loop(0, TALL, regrid_row, 0)
        regrid_edges()
        wait_arrivals(functools.partial(x_copy, s), ring)

        pos = lane80 & 3
        pos8 = lane8 & 3
        own = eg[s]
        for t in (0, 1, 18, 19):
            own = jnp.where((lane80 >> 2) == t, pltpu.roll(xr[s, t], 4 * t + 2, 1), own)
        beside = jnp.where(pos < 2, eg_recv[s, 0], eg_recv[s, 1])
        pos16 = lane16 & 3
        corners = [jnp.where(pos16 < 2, cp_recv[s, n, 0], cp_recv[s, n, 1]) for n in range(2)]
        corner = jnp.where(lane16 < 64, corners[0], corners[1])
        corner = jnp.concatenate(
            [pltpu.roll(corner, LANES - 8 * part, 1) if part else corner for part in range(5)], 0
        )
        beside = jnp.where((lane80 >= 8) & (lane80 < 72), beside, corner)

        def taps(halo, mine, where):
            return (
                pltpu.roll(jnp.where(where == 0, halo, mine), 1, 1),
                halo,
                pltpu.roll(jnp.where(where == 2, mine, halo), LANES - 1, 1),
            )

        def swapped(halo, where):
            return jnp.where(where == 1, pltpu.roll(halo, LANES - 1, 1), pltpu.roll(halo, 1, 1))

        state_taps = taps(beside, own, pos)
        for b in range(3):
            x3e[CH * b : CH * b + CH] = state_taps[b]
        hh[...] = swapped(beside, pos)

        def add(t, acc):
            return jnp.where((lane8 >> 2) == t, pltpu.roll(fr[t], 4 * t + 2, 1), acc)

        own_forcing = lax.fori_loop(0, TALL, add, jnp.zeros((8, LANES), F32), unroll=4)
        beside_forcing = fr[TALL]
        first, second, third = taps(beside_forcing, own_forcing, pos8)
        ones = jnp.where(sub8 < 7, 1.0, 0.0)
        x3e[240:256] = jnp.concatenate(
            [jnp.where(low, first, second), jnp.where(low, third, ones)], 0
        ).astype(BF)
        swapped_forcing = swapped(beside_forcing, pos8)

        def widen(t, c):
            forcing = fr[t]
            turned = pltpu.roll(swapped_forcing, 126 - 4 * t, 1)
            left = jnp.where(lane8 == 0, turned, pltpu.roll(forcing, 1, 1))
            right = jnp.where(lane8 == LANES - 1, turned, pltpu.roll(forcing, LANES - 1, 1))
            x3[t, 240:256] = jnp.concatenate(
                [jnp.where(low, left, forcing), jnp.where(low, right, ones)], 0
            ).astype(BF)
            cells = xr[s, t]
            turned = pltpu.roll(hh[...], 126 - 4 * t, 1)
            x3[t, 0:80] = jnp.where(lane80 == 0, turned, pltpu.roll(cells, 1, 1))
            x3[t, 80:160] = cells
            x3[t, 160:240] = jnp.where(
                lane80 == LANES - 1, turned, pltpu.roll(cells, LANES - 1, 1)
            )
            return c

        lax.fori_loop(0, TALL, widen, 0, unroll=2)

        def first_conv(p, c):
            h = 2 * p
            total = jnp.zeros((HOP, 256), F32)
            for a in range(3):
                columns = jnp.concatenate([x3[h + a], x3[h + a + 1]], 1)
                total = total + jnp.dot(w1[a], columns, preferred_element_type=F32)
            active = gelu(total).astype(BF)
            hid[h] = active[:, 0:128]
            hid[h + 1] = active[:, 128:256]
            return c

        lax.fori_loop(0, 9, first_conv, 0)

        @pl.when(i == 0)
        def _():
            hid[0] = jnp.zeros((HOP, LANES), BF)

        @pl.when(i == lats - 1)
        def _():
            hid[17] = jnp.zeros((HOP, LANES), BF)

        total = jnp.zeros((HOP, LANES), F32)
        for a in range(3):
            columns = x3e[...]
            if a:
                columns = pltpu.roll(columns, LANES - 4 * a, 1)
            total = total + jnp.dot(w1[a], columns, preferred_element_type=F32)
        slot = iota((HOP, LANES), 1) >> 2
        outside = ((slot == 0) & (i == 0)) | ((slot == 17) & (i == lats - 1))
        he[...] = jnp.where(outside, 0.0, gelu(total)).astype(BF)
        total = jnp.zeros((240, LANES), F32)
        for a in range(3):
            columns = he[...]
            if a:
                columns = pltpu.roll(columns, LANES - 4 * a, 1)
            total = total + jnp.dot(w2[a], columns, preferred_element_type=F32)
        ze[...] = jnp.where(
            pos == 1,
            pltpu.roll(total[160:240], LANES - 1, 1),
            pltpu.roll(total[0:80], 1, 1),
        )

        def second_conv(p, c):
            r = 2 * p
            total = jnp.zeros((240, 256), F32)
            for a in range(3):
                columns = jnp.concatenate([hid[r + a], hid[r + a + 1]], 1)
                total = total + jnp.dot(w2[a], columns, preferred_element_type=F32)
            for u in range(2):
                part = total[:, 128 * u : 128 * u + 128]
                turned = pltpu.roll(ze[...], 126 - 4 * (r + u), 1)
                left = jnp.where(lane80 == 0, turned, pltpu.roll(part[0:80], 1, 1))
                right = jnp.where(
                    lane80 == LANES - 1, turned, pltpu.roll(part[160:240], LANES - 1, 1)
                )
                update = left + part[80:160] + right
                new = xr[s, r + u + 2].astype(F32) + wet[pl.ds(r + u, 1), :] * update
                finish_row(s, r + u, new)
            return c

        lax.fori_loop(0, ROWS // 2, second_conv, 0)

    for s in range(STEPS):
        if s:
            surface(s)
            start_all(functools.partial(s_copy, s), around)

            @pl.when(ocean)
            def _(s=s):
                edges(s)
                start_all(functools.partial(x_copy, s), ring)

        wait_arrivals(functools.partial(s_copy, s), around)
        sources(s)

        @pl.when(ocean)
        def _(s=s):
            ocean_step(s)

        @pl.when(air)
        def _(s=s):
            air_step(s)

    out_ref[0] = flip[...].reshape(CH, ROWS, LANES).astype(BF)

    for s in range(STEPS):
        wait_departures(functools.partial(s_copy, s), around)

    @pl.when(ocean)
    def _():
        for s in range(STEPS):
            wait_departures(functools.partial(x_copy, s), ring)
        wait_departures(q_copy, ring)


def solution(mesh):
    lats, lons = mesh.shape["lat"], mesh.shape["lon"]
    vmem = pl.BlockSpec(memory_space=pltpu.VMEM)
    anywhere = pl.BlockSpec(memory_space=pl.ANY)
    dma = pltpu.SemaphoreType.DMA

    def local(*args):
        return pl.pallas_call(
            functools.partial(kernel, lats, lons),
            out_shape=jax.ShapeDtypeStruct((1, CH, ROWS, LANES), BF),
            in_specs=[vmem] * 8 + [anywhere, vmem, anywhere],
            out_specs=vmem,
            scratch_shapes=[
                pltpu.VMEM((CH * ROWS, LANES), F32),
                pltpu.VMEM((STEPS, TALL, CH, LANES), BF),
                pltpu.VMEM((STEPS, CH, LANES), BF),
                pltpu.VMEM((STEPS, 2, CH, LANES), BF),
                pltpu.VMEM((STEPS, 16, LANES), BF),
                pltpu.VMEM((STEPS, 2, 2, 16, LANES), BF),
                pltpu.VMEM((STEPS, 64, LANES), BF),
                pltpu.VMEM((STEPS, 160, LANES), BF),
                pltpu.VMEM((STEPS, 16, LANES), BF),
                pltpu.VMEM((STEPS, 3, 2, 16, LANES), BF),
                pltpu.VMEM((TALL, 8, LANES), F32),
                pltpu.VMEM((8, LANES), F32),
                pltpu.VMEM((3, 2, 8, LANES), F32),
                pltpu.VMEM((TALL + 1, 2, 8, LANES), I32),
                pltpu.VMEM((TALL + 1, 2, 8, LANES), I32),
                pltpu.VMEM((TALL + 1, 2, 8, LANES), F32),
                pltpu.VMEM((40, 2, 8, LANES), F32),
                pltpu.VMEM((TALL + 1, 8, LANES), F32),
                pltpu.VMEM((TALL, 256, LANES), BF),
                pltpu.VMEM((256, LANES), BF),
                pltpu.VMEM((3, HOP, 256), BF),
                pltpu.VMEM((3, 240, HOP), BF),
                pltpu.VMEM((384, 96), BF),
                pltpu.VMEM((18, HOP, LANES), BF),
                pltpu.VMEM((HOP, LANES), BF),
                pltpu.VMEM((CH, LANES), BF),
                pltpu.VMEM((CH, LANES), F32),
                pltpu.VMEM((64, LANES), F32),
                pltpu.VMEM((ROWS, LANES), F32),
                pltpu.VMEM((24, CH), BF),
                pltpu.VMEM((HO, 9, 84), BF),
                pltpu.VMEM((CH, 9, HO), BF),
                pltpu.VMEM((16 * HOP, LANES), F32),
                pltpu.VMEM((2, 16 * CH, LANES), F32),
                dma((2,)),
                dma((STEPS, 3, 3)),
                dma((STEPS, 3, 3)),
                dma((STEPS, 3, 3)),
                dma((STEPS, 3, 3)),
                dma((3, 3)),
                dma((3, 3)),
            ],
            compiler_params=pltpu.CompilerParams(
                collective_id=0,
                has_side_effects=True,
                vmem_limit_bytes=48 * 1024 * 1024,
            ),
        )(*args)

    return jax.shard_map(
        local,
        mesh=mesh,
        in_specs=(
            P("grp", None, "lat", "lon"),
            P("lat", "lon"),
            P("grp", None, None, "lat", "lon"),
            P("grp", None, "lat", "lon"),
            P(),
            P(),
            P(),
            P(),
            P(),
            P(),
            P(),
        ),
        out_specs=P("grp", None, "lat", "lon"),
        check_vma=False,
    )
```

profile of v0, /device:TPU:102, one launch (start us, length us, event | category | flops | bytes accessed | tf_op | source)
XLA Modules:
  0.0 45.1 jit_solution(6080490683801109992)
XLA Ops:
  0.0 1.0 %copy.12.atm_in_ref = bf16[384,84]{1,0:T(8,128)(2,1)S(1)} copy(bf16[384,84]{0,1:T(8,128)(2,1)} %param.16) | data formatting | bytes 129024 | tf_op args[5]
  1.0 0.0 copy-start.8
  1.0 1.2 %copy.14.ocn_out_hbm = bf16[80,9,200]{2,1,0:T(8,128)(2,1)S(1)} copy(bf16[80,9,200]{2,0,1:T(8,128)(2,1)} %param.21) | data formatting | bytes 576000 | tf_op args[10]
  2.2 0.0 copy-done.8
  2.2 0.0 copy-start
  2.2 0.0 copy-start.1
  2.2 0.0 copy-start.2
  2.3 0.0 copy-start.3
  2.3 0.0 copy-start.4
  2.3 0.0 copy-start.5
  2.3 0.0 copy-start.6
  2.3 0.0 copy-start.7
  2.3 0.7 %copy.13.ocn_in_hbm = bf16[200,9,84]{2,1,0:T(8,128)(2,1)S(1)} copy(bf16[200,9,84]{0,2,1:T(8,128)(2,1)S(1)} %copy-done.8) | data formatting | bytes 604800 | tf_op args[8]
  3.1 0.1 copy-done
  3.2 0.0 copy-done.1
  3.2 0.0 copy-done.2
  3.2 0.0 copy-done.3
  3.2 0.0 copy-done.4
  3.2 0.0 copy-done.5
  3.2 0.0 copy-done.6
  3.2 0.0 copy-done.7
  3.2 41.1 %shard_map.109 = bf16[1,80,16,128]{3,2,1,0:T(8,128)(2,1)S(1)} custom-call(bf16[1,80,16,128]{3,2,1,0:T(8,128)(2,1)S(1)} %copy-done, s32[16,128]{1,0:T(8,128)S(1)} %copy-done.4, s32[1,2,4,16,128]{4,3,2,1,0:T(8,128)S(1)} %copy-done.1, f32[1,4,16,128]{3,2,1,0:T(8,128)S(1)} %copy-done.3, f32[2,4,80]{2,1,0:T(4,128)S(1)} %copy-done.5, ...), custom_call_target="tpu_custom_call" | custom-call | tf_op jit(solution)/shard_map/pallas_call | solution.py:663
  44.4 0.7 %copy.16 = bf16[1,80,16,128]{3,2,1,0:T(8,128)(2,1)} copy(bf16[1,80,16,128]{3,2,1,0:T(8,128)(2,1)S(1)} %shard_map.109) | data formatting | bytes 655360
Async XLA Ops:
  1.0 1.2 %copy-start.8 = (bf16[200,9,84]{0,2,1:T(8,128)(2,1)S(1)}, bf16[200,9,84]{0,2,1:T(8,128)(2,1)}, u32[]{:S(2)}) copy-start(bf16[200,9,84]{0,2,1:T(8,128)(2,1)} %param.19) | copy-start | bytes 907204
  2.2 1.0 %copy-start = (bf16[1,80,16,128]{3,2,1,0:T(8,128)(2,1)S(1)}, bf16[1,80,16,128]{3,2,1,0:T(8,128)(2,1)}, u32[]{:S(2)}) copy-start(bf16[1,80,16,128]{3,2,1,0:T(8,128)(2,1)} %state_ref.1) | copy-start | bytes 983044
  2.2 1.0 %copy-start.1 = (s32[1,2,4,16,128]{4,3,2,1,0:T(8,128)S(1)}, s32[1,2,4,16,128]{4,3,2,1,0:T(8,128)}, u32[]{:S(2)}) copy-start(s32[1,2,4,16,128]{4,3,2,1,0:T(8,128)} %offsets_ref.1) | copy-start | bytes 196612
  2.2 1.0 %copy-start.2 = (bf16[80,384]{1,0:T(8,128)(2,1)S(1)}, bf16[80,384]{1,0:T(8,128)(2,1)}, u32[]{:S(2)}) copy-start(bf16[80,384]{1,0:T(8,128)(2,1)} %atm_out_ref.1) | copy-start | bytes 184324
  2.3 0.9 %copy-start.3 = (f32[1,4,16,128]{3,2,1,0:T(8,128)S(1)}, f32[1,4,16,128]{3,2,1,0:T(8,128)}, u32[]{:S(2)}) copy-start(f32[1,4,16,128]{3,2,1,0:T(8,128)} %weights_ref.1) | copy-start | bytes 98308
  2.3 0.9 %copy-start.4 = (s32[16,128]{1,0:T(8,128)S(1)}, s32[16,128]{1,0:T(8,128)}, u32[]{:S(2)}) copy-start(s32[16,128]{1,0:T(8,128)} %mask_ref.1) | copy-start | bytes 24580
  2.3 0.9 %copy-start.5 = (f32[2,4,80]{2,1,0:T(4,128)S(1)}, f32[2,4,80]{2,1,0:T(4,128)}, u32[]{:S(2)}) copy-start(f32[2,4,80]{2,1,0:T(4,128)} %proj_ref.1) | copy-start | bytes 7684
  2.3 0.9 %copy-start.6 = (f32[384]{0:T(512)S(1)}, f32[384]{0:T(512)}, u32[]{:S(2)}) copy-start(f32[384]{0:T(512)} %atm_bias_ref.1) | copy-start | bytes 4612
  2.3 0.9 %copy-start.7 = (f32[200]{0:T(256)S(1)}, f32[200]{0:T(256)}, u32[]{:S(2)}) copy-start(f32[200]{0:T(256)} %ocn_bias_ref.1) | copy-start | bytes 2404
where the time goes:
time: 45.2 us; the launch traced here: 45.1 us
  Pallas kernels  41.1 us (91%)
  local copies, waits for them, and re-layouts  3.85 us (9%)
    pallas_call x1, Pallas kernels, local(): pl.pallas_call(functools.partial(kernel, lats, lons), out_shape=jax.Shape...  41.1 us
    unnamed x22, local copies, waits for them, and re-layouts  3.85 us

commit v1 on v0

--- a/solution.py
+++ b/solution.py
@@ -26,10 +26,6 @@
     return lax.broadcasted_iota(I32, shape, axis)
 
 
-def one_hot(shape, test):
-    return jnp.where(test, 1.0, 0.0).astype(F32).astype(BF)
-
-
 def gelu(x):
     inner = x * (0.7978845608028654 + 0.035677408136300125 * (x * x))
     half = 0.5 * x
@@ -40,13 +36,6 @@
     high = x.astype(BF).astype(F32)
     middle = (x - high).astype(BF).astype(F32)
     return high, middle, x - high - middle
-
-
-def bias_columns(bias, rows):
-    count = bias.shape[0]
-    spread = jnp.broadcast_to(bias.reshape(1, count), (rows, count))
-    same = iota((rows, count), 0) == iota((rows, count), 1)
-    return thirds(jnp.sum(jnp.where(same, spread, 0.0), axis=1, keepdims=True))
 
 
 def kernel(
@@ -96,8 +85,6 @@
     pp,
     ocn_in_v,
     ocn_out_v,
-    wt1,
-    wt2,
     load_sem,
     s_send,
     s_recv,
@@ -321,55 +308,32 @@
         for load in loads:
             load.wait()
 
-        def widen1(o, c):
-            wt1[pl.ds(pl.multiple_of(16 * o, 16), 9), 0:84] = ocn_in_v[o].astype(F32)
-            return c
-
-        lax.fori_loop(0, HO, widen1, 0, unroll=8)
-        wt1[16 * HO :, :] = jnp.zeros((16 * (HOP - HO), LANES), F32)
-        wt2[1] = jnp.zeros((16 * CH, LANES), F32)
-
-        def widen2(o, c):
-            taps = ocn_out_v[o].astype(F32)
-            wt2[0, pl.ds(pl.multiple_of(16 * o, 16), 9), :] = taps[:, 0:128]
-            wt2[1, pl.ds(pl.multiple_of(16 * o, 16), 9), 0 : HO - 128] = taps[:, 128:HO]
-            return c
-
-        lax.fori_loop(0, CH, widen2, 0, unroll=8)
-        channel = iota((84, 256), 0)
-        lane = iota((84, 256), 1)
-        bias = bias_columns(ocn_bias_ref[...], HOP)
-        lane_w = iota((HOP, 256), 1)
+        def rows_of(values):
+            return thirds(values.reshape(1, -1))
+
+        spare = jnp.zeros((1, HO), F32)
+        bias = jnp.concatenate([*rows_of(ocn_bias_ref[...]), spare], 0)
         for a in range(3):
-            total = jnp.zeros((HOP, 256), F32)
+            taps = [ocn_in_v[3 * a + b].astype(F32) for b in range(3)]
+            last = bias if a == 1 else jnp.zeros((4, HO), F32)
+            stacked = jnp.concatenate(
+                [tap[0:CH] for tap in taps] + [tap[CH:] for tap in taps] + [last], 0
+            )
+            stacked = jnp.concatenate([stacked, jnp.zeros((256, 256 - HO), F32)], 1)
+            w1[a] = stacked.T[0:HOP].astype(BF)
             for b in range(3):
-                target = jnp.where(channel < CH, channel + CH * b, channel + 240 + 4 * b - CH)
-                total = total + jnp.dot(
-                    wt1[pl.ds(3 * a + b, HOP, stride=16), 0:84].astype(BF),
-                    one_hot((84, 256), lane == target),
-                    preferred_element_type=F32,
-                )
-            if a == 1:
-                for part in range(3):
-                    total = jnp.where(lane_w == 252 + part, bias[part], total)
-            w1[a] = total.astype(BF)
-            for b in range(3):
-                rows = pl.ds(3 * a + b, CH, stride=16)
-                halves = [wt2[half, rows, :].astype(BF) for half in range(2)]
-                w2[a, CH * b : CH * b + CH, :] = jnp.concatenate(halves, 1)[:, 0:HOP]
+                values = ocn_out_v[3 * a + b].astype(F32)
+                w2[a, CH * b : CH * b + CH, :] = jnp.concatenate(
+                    [values, jnp.zeros((CH, HOP - HO), F32)], 1
+                ).astype(BF)
 
     @pl.when(air)
     def _():
-        total = jnp.dot(
-            atm_in_ref[...],
-            one_hot((84, 96), iota((84, 96), 0) == iota((84, 96), 1)),
-            preferred_element_type=F32,
+        bias = thirds(atm_bias_ref[...].reshape(1, -1))
+        stacked = jnp.concatenate(
+            [atm_in_ref[...].astype(F32), *bias, jnp.zeros((41, 384), F32)], 0
         )
-        bias = bias_columns(atm_bias_ref[...], 384)
-        lane = iota((384, 96), 1)
-        for part in range(3):
-            total = jnp.where(lane == 84 + part, bias[part], total)
-        wa[...] = total.astype(BF)
+        wa[...] = stacked.T[:, 0:96].astype(BF)
 
     def decode(values, t, column, row):
         for kp in range(2):
@@ -660,6 +624,10 @@
     dma = pltpu.SemaphoreType.DMA
 
     def local(*args):
+        args = list(args)
+        args[5] = args[5].T
+        args[8] = args[8].transpose(1, 2, 0)
+        args[10] = args[10].transpose(1, 0, 2)
         return pl.pallas_call(
             functools.partial(kernel, lats, lons),
             out_shape=jax.ShapeDtypeStruct((1, CH, ROWS, LANES), BF),
@@ -696,10 +664,8 @@
                 pltpu.VMEM((64, LANES), F32),
                 pltpu.VMEM((ROWS, LANES), F32),
                 pltpu.VMEM((24, CH), BF),
-                pltpu.VMEM((HO, 9, 84), BF),
-                pltpu.VMEM((CH, 9, HO), BF),
-                pltpu.VMEM((16 * HOP, LANES), F32),
-                pltpu.VMEM((2, 16 * CH, LANES), F32),
+                pltpu.VMEM((9, 84, HO), BF),
+                pltpu.VMEM((9, CH, HO), BF),
                 dma((2,)),
                 dma((STEPS, 3, 3)),
                 dma((STEPS, 3, 3)),

time: 45.2 us -> 50.6 us (1.12)
  local copies, waits for them, and re-layouts: 3.85 us -> 9.06 us
    unnamed x22 -> x23, local copies, waits for them, and re-layouts: 3.85 us -> 9.06 us
where the time goes in v1:
time: 50.6 us; the launch traced here: 50.1 us
  Pallas kernels  41 us (81%)
  local copies, waits for them, and re-layouts  9.06 us (18%)
    pallas_call x1, Pallas kernels, local(): pl.pallas_call(functools.partial(kernel, lats, lons), out_shape=jax.Shape...  41 us
    unnamed x23, local copies, waits for them, and re-layouts  9.06 us

profile of v1, /device:TPU:102, one launch (start us, length us, event | category | flops | bytes accessed | tf_op | source)
XLA Modules:
  0.0 50.1 jit_solution(2554484290727165653)
XLA Ops:
  0.0 0.0 copy-start.8
  0.0 0.0 copy-start.10
  0.0 0.7 %copy-done.8 = f32[2,4,80]{2,1,0:T(4,128)S(1)} copy-done((f32[2,4,80]{2,1,0:T(4,128)S(1)}, f32[2,4,80]{2,1,0:T(4,128)}, u32[]{:S(2)}) %copy-start.8) | copy-done | bytes 2584
  0.7 0.0 copy-done.10
  0.7 0.0 copy-start
  0.7 1.0 %copy-done = bf16[200,9,84]{0,2,1:T(8,128)(2,1)S(1)} copy-done((bf16[200,9,84]{0,2,1:T(8,128)(2,1)S(1)}, bf16[200,9,84]{0,2,1:T(8,128)(2,1)}, u32[]{:S(2)}) %copy-start) | copy-done | bytes 302424
  1.7 0.0 copy-start.1
  1.7 1.0 %copy-done.1 = bf16[80,9,200]{2,0,1:T(8,128)(2,1)S(1)} copy-done((bf16[80,9,200]{2,0,1:T(8,128)(2,1)S(1)}, bf16[80,9,200]{2,0,1:T(8,128)(2,1)}, u32[]{:S(2)}) %copy-start.1) | copy-done | bytes 288024
  2.7 0.0 copy-start.2
  2.7 1.0 %copy-done.2 = bf16[1,80,16,128]{3,2,1,0:T(8,128)(2,1)S(1)} copy-done((bf16[1,80,16,128]{3,2,1,0:T(8,128)(2,1)S(1)}, bf16[1,80,16,128]{3,2,1,0:T(8,128)(2,1)}, u32[]{:S(2)}) %copy-start.2) | copy-done | bytes 327704
  3.7 0.0 copy-start.3
  3.7 0.9 %copy-done.3 = bf16[384,84]{0,1:T(8,128)(2,1)S(1)} copy-done((bf16[384,84]{0,1:T(8,128)(2,1)S(1)}, bf16[384,84]{0,1:T(8,128)(2,1)}, u32[]{:S(2)}) %copy-start.3) | copy-done | bytes 64536
  4.5 0.0 copy-start.4
  4.5 0.8 %copy-done.4 = s32[1,2,4,16,128]{4,3,2,1,0:T(8,128)S(1)} copy-done((s32[1,2,4,16,128]{4,3,2,1,0:T(8,128)S(1)}, s32[1,2,4,16,128]{4,3,2,1,0:T(8,128)}, u32[]{:S(2)}) %copy-start.4) | copy-done | bytes 65560
  5.4 0.0 copy-start.5
  5.4 0.8 %copy-done.5 = bf16[80,384]{1,0:T(8,128)(2,1)S(1)} copy-done((bf16[80,384]{1,0:T(8,128)(2,1)S(1)}, bf16[80,384]{1,0:T(8,128)(2,1)}, u32[]{:S(2)}) %copy-start.5) | copy-done | bytes 61464
  6.2 0.0 copy-start.6
  6.2 0.8 %copy-done.6 = f32[1,4,16,128]{3,2,1,0:T(8,128)S(1)} copy-done((f32[1,4,16,128]{3,2,1,0:T(8,128)S(1)}, f32[1,4,16,128]{3,2,1,0:T(8,128)}, u32[]{:S(2)}) %copy-start.6) | copy-done | bytes 32792
  7.0 0.0 copy-start.7
  7.0 0.7 %copy-done.7 = s32[16,128]{1,0:T(8,128)S(1)} copy-done((s32[16,128]{1,0:T(8,128)S(1)}, s32[16,128]{1,0:T(8,128)}, u32[]{:S(2)}) %copy-start.7) | copy-done | bytes 8216
  7.7 0.0 copy-start.9
  7.7 0.7 %copy-done.9 = f32[384]{0:T(512)S(1)} copy-done((f32[384]{0:T(512)S(1)}, f32[384]{0:T(512)}, u32[]{:S(2)}) %copy-start.9) | copy-done | bytes 1560
  8.3 41.0 %shard_map.109 = bf16[1,80,16,128]{3,2,1,0:T(8,128)(2,1)S(1)} custom-call(bf16[1,80,16,128]{3,2,1,0:T(8,128)(2,1)S(1)} %copy-done.2, s32[16,128]{1,0:T(8,128)S(1)} %copy-done.7, s32[1,2,4,16,128]{4,3,2,1,0:T(8,128)S(1)} %copy-done.4, f32[1,4,16,128]{3,2,1,0:T(8,128)S(1)} %copy-done.6, f32[2,4,80]{2,1,0:T(4,128)S(1)} %copy-done.8, ...), custom_call_target="tpu_custom_call" | custom-call | tf_op jit(solution)/shard_map/pallas_call | solution.py:631
  49.4 0.7 %copy.13 = bf16[1,80,16,128]{3,2,1,0:T(8,128)(2,1)} copy(bf16[1,80,16,128]{3,2,1,0:T(8,128)(2,1)S(1)} %shard_map.109) | data formatting | bytes 655360
Async XLA Ops:
  0.0 0.7 %copy-start.8 = (f32[2,4,80]{2,1,0:T(4,128)S(1)}, f32[2,4,80]{2,1,0:T(4,128)}, u32[]{:S(2)}) copy-start(f32[2,4,80]{2,1,0:T(4,128)} %proj_ref.1) | copy-start | bytes 7684
  0.0 0.7 %copy-start.10 = (f32[200]{0:T(256)S(1)}, f32[200]{0:T(256)}, u32[]{:S(2)}) copy-start(f32[200]{0:T(256)} %ocn_bias_ref.1) | copy-start | bytes 2404
  0.7 1.0 %copy-start = (bf16[200,9,84]{0,2,1:T(8,128)(2,1)S(1)}, bf16[200,9,84]{0,2,1:T(8,128)(2,1)}, u32[]{:S(2)}) copy-start(bf16[200,9,84]{0,2,1:T(8,128)(2,1)} %param.19) | copy-start | bytes 907204
  1.7 1.0 %copy-start.1 = (bf16[80,9,200]{2,0,1:T(8,128)(2,1)S(1)}, bf16[80,9,200]{2,0,1:T(8,128)(2,1)}, u32[]{:S(2)}) copy-start(bf16[80,9,200]{2,0,1:T(8,128)(2,1)} %param.21) | copy-start | bytes 864004
  2.7 1.0 %copy-start.2 = (bf16[1,80,16,128]{3,2,1,0:T(8,128)(2,1)S(1)}, bf16[1,80,16,128]{3,2,1,0:T(8,128)(2,1)}, u32[]{:S(2)}) copy-start(bf16[1,80,16,128]{3,2,1,0:T(8,128)(2,1)} %state_ref.1) | copy-start | bytes 983044
  3.7 0.9 %copy-start.3 = (bf16[384,84]{0,1:T(8,128)(2,1)S(1)}, bf16[384,84]{0,1:T(8,128)(2,1)}, u32[]{:S(2)}) copy-start(bf16[384,84]{0,1:T(8,128)(2,1)} %param.16) | copy-start | bytes 193540
  4.5 0.8 %copy-start.4 = (s32[1,2,4,16,128]{4,3,2,1,0:T(8,128)S(1)}, s32[1,2,4,16,128]{4,3,2,1,0:T(8,128)}, u32[]{:S(2)}) copy-start(s32[1,2,4,16,128]{4,3,2,1,0:T(8,128)} %offsets_ref.1) | copy-start | bytes 196612
  5.4 0.8 %copy-start.5 = (bf16[80,384]{1,0:T(8,128)(2,1)S(1)}, bf16[80,384]{1,0:T(8,128)(2,1)}, u32[]{:S(2)}) copy-start(bf16[80,384]{1,0:T(8,128)(2,1)} %atm_out_ref.1) | copy-start | bytes 184324
  6.2 0.8 %copy-start.6 = (f32[1,4,16,128]{3,2,1,0:T(8,128)S(1)}, f32[1,4,16,128]{3,2,1,0:T(8,128)}, u32[]{:S(2)}) copy-start(f32[1,4,16,128]{3,2,1,0:T(8,128)} %weights_ref.1) | copy-start | bytes 98308
  7.0 0.7 %copy-start.7 = (s32[16,128]{1,0:T(8,128)S(1)}, s32[16,128]{1,0:T(8,128)}, u32[]{:S(2)}) copy-start(s32[16,128]{1,0:T(8,128)} %mask_ref.1) | copy-start | bytes 24580
  7.7 0.7 %copy-start.9 = (f32[384]{0:T(512)S(1)}, f32[384]{0:T(512)}, u32[]{:S(2)}) copy-start(f32[384]{0:T(512)} %atm_bias_ref.1) | copy-start | bytes 4612

commit v2 on v1

--- a/solution.py
+++ b/solution.py
@@ -41,6 +41,18 @@
 def kernel(
     lats,
     lons,
+    state_hbm,
+    mask_hbm,
+    offsets_hbm,
+    weights_hbm,
+    proj_hbm,
+    atm_in_hbm,
+    atm_bias_hbm,
+    atm_out_hbm,
+    ocn_in_hbm,
+    ocn_bias_hbm,
+    ocn_out_hbm,
+    out_ref,
     state_ref,
     mask_ref,
     offsets_ref,
@@ -49,10 +61,9 @@
     atm_in_ref,
     atm_bias_ref,
     atm_out_ref,
-    ocn_in_hbm,
+    ocn_in_v,
     ocn_bias_ref,
-    ocn_out_hbm,
-    out_ref,
+    ocn_out_v,
     flip,
     xr,
     eg,
@@ -83,8 +94,6 @@
     keep,
     wet,
     pp,
-    ocn_in_v,
-    ocn_out_v,
     load_sem,
     s_send,
     s_recv,
@@ -115,14 +124,33 @@
     lane80 = iota((CH, LANES), 1)
     lane16 = iota((16, LANES), 1)
 
+    pairs = (
+        (state_hbm, state_ref),
+        (mask_hbm, mask_ref),
+        (offsets_hbm, offsets_ref),
+        (weights_hbm, weights_ref),
+        (proj_hbm, proj_ref),
+        (atm_in_hbm, atm_in_ref),
+        (atm_bias_hbm, atm_bias_ref),
+        (atm_out_hbm, atm_out_ref),
+        (ocn_in_hbm, ocn_in_v),
+        (ocn_bias_hbm, ocn_bias_ref),
+        (ocn_out_hbm, ocn_out_v),
+    )
     loads = [
-        pltpu.make_async_copy(ocn_in_hbm, ocn_in_v, load_sem.at[0]),
-        pltpu.make_async_copy(ocn_out_hbm, ocn_out_v, load_sem.at[1]),
+        pltpu.make_async_copy(src, dst, load_sem.at[n]) for n, (src, dst) in enumerate(pairs)
     ]
+    for load in loads[0:5]:
+        load.start()
 
     @pl.when(ocean)
     def _():
-        for load in loads:
+        for load in loads[8:11]:
+            load.start()
+
+    @pl.when(air)
+    def _():
+        for load in loads[5:8]:
             load.start()
 
     for di, block, rows in ((-1, 0, slice(0, 2)), (1, 2, slice(18, 20))):
@@ -216,6 +244,7 @@
         for di, dj in pairs:
             when(has[di], lambda di=di, dj=dj: make(di, dj).wait_send())
 
+    loads[0].wait()
     flip[...] = state_ref[0].astype(F32).reshape(CH * ROWS, LANES)
 
     def to_rows(r, c):
@@ -224,6 +253,8 @@
 
     lax.fori_loop(0, ROWS, to_rows, 0, unroll=4)
 
+    loads[1].wait()
+    loads[4].wait()
     wet_values = mask_ref[...].astype(F32)
     wet[...] = wet_values
     kept = jnp.where(ocean, wet_values, 1.0)
@@ -277,6 +308,8 @@
 
     surface(0)
 
+    loads[2].wait()
+    loads[3].wait()
     for k in range(4):
         code = (offsets_ref[0, 0, k] + HW) * 32 + (offsets_ref[0, 1, k] + HW)
         flip[16 * k : 16 * k + 16] = code.astype(F32)
@@ -305,7 +338,7 @@
 
     @pl.when(ocean)
     def _():
-        for load in loads:
+        for load in loads[8:11]:
             load.wait()
 
         def rows_of(values):
@@ -329,6 +362,8 @@
 
     @pl.when(air)
     def _():
+        for load in loads[5:8]:
+            load.wait()
         bias = thirds(atm_bias_ref[...].reshape(1, -1))
         stacked = jnp.concatenate(
             [atm_in_ref[...].astype(F32), *bias, jnp.zeros((41, 384), F32)], 0
@@ -631,9 +666,20 @@
         return pl.pallas_call(
             functools.partial(kernel, lats, lons),
             out_shape=jax.ShapeDtypeStruct((1, CH, ROWS, LANES), BF),
-            in_specs=[vmem] * 8 + [anywhere, vmem, anywhere],
+            in_specs=[anywhere] * 11,
             out_specs=vmem,
             scratch_shapes=[
+                pltpu.VMEM((1, CH, ROWS, LANES), BF),
+                pltpu.VMEM((ROWS, LANES), I32),
+                pltpu.VMEM((1, 2, 4, ROWS, LANES), I32),
+                pltpu.VMEM((1, 4, ROWS, LANES), F32),
+                pltpu.VMEM((2, 4, CH), F32),
+                pltpu.VMEM((84, 384), BF),
+                pltpu.VMEM((384,), F32),
+                pltpu.VMEM((CH, 384), BF),
+                pltpu.VMEM((9, 84, HO), BF),
+                pltpu.VMEM((HO,), F32),
+                pltpu.VMEM((9, CH, HO), BF),
                 pltpu.VMEM((CH * ROWS, LANES), F32),
                 pltpu.VMEM((STEPS, TALL, CH, LANES), BF),
                 pltpu.VMEM((STEPS, CH, LANES), BF),
@@ -664,9 +710,7 @@
                 pltpu.VMEM((64, LANES), F32),
                 pltpu.VMEM((ROWS, LANES), F32),
                 pltpu.VMEM((24, CH), BF),
-                pltpu.VMEM((9, 84, HO), BF),
-                pltpu.VMEM((9, CH, HO), BF),
-                dma((2,)),
+                dma((11,)),
                 dma((STEPS, 3, 3)),
                 dma((STEPS, 3, 3)),
                 dma((STEPS, 3, 3)),
@@ -677,7 +721,7 @@
             compiler_params=pltpu.CompilerParams(
                 collective_id=0,
                 has_side_effects=True,
-                vmem_limit_bytes=48 * 1024 * 1024,
+                vmem_limit_bytes=60 * 1024 * 1024,
             ),
         )(*args)
 

time: 50.6 us -> 43.2 us (0.85)
  local copies, waits for them, and re-layouts: 9.06 us -> 1.72 us
    unnamed x23 -> x1, local copies, waits for them, and re-layouts: 9.06 us -> 1.72 us
where the time goes in v2:
time: 43.2 us; the launch traced here: 43.1 us
  Pallas kernels  41.4 us (96%)
  local copies, waits for them, and re-layouts  1.72 us (4%)
    pallas_call x1, Pallas kernels, local(): pl.pallas_call(functools.partial(kernel, lats, lons), out_shape=jax.Shape...  41.4 us
    unnamed x1, local copies, waits for them, and re-layouts  1.72 us

profile of v2, /device:TPU:102, one launch (start us, length us, event | category | flops | bytes accessed | tf_op | source)
XLA Modules:
  0.0 43.1 jit_solution(14652351112653682161)
XLA Ops:
  0.0 41.4 %shard_map.109 = bf16[1,80,16,128]{3,2,1,0:T(8,128)(2,1)} custom-call(bf16[1,80,16,128]{3,2,1,0:T(8,128)(2,1)} %state_hbm.1, s32[16,128]{1,0:T(8,128)} %mask_hbm.1, s32[1,2,4,16,128]{4,3,2,1,0:T(8,128)} %offsets_hbm.1, f32[1,4,16,128]{3,2,1,0:T(8,128)} %weights_hbm.1, f32[2,4,80]{2,1,0:T(4,128)} %proj_hbm.1, bf16[84,384]{1,0:T(8,128)(2,1)} %bitcast.5, ...), custom_call_target="tpu_custom_call" | custom-call | tf_op jit(solution)/shard_map/pallas_call | solution.py:666
  41.4 1.7 %copy.13 = bf16[1,80,16,128]{3,2,1,0:T(8,128)(2,1)} copy(bf16[1,80,16,128]{3,2,1,0:T(8,128)(2,1)} %shard_map.109) | data formatting | bytes 655360

commit v3 on v2

--- a/solution.py
+++ b/solution.py
@@ -70,6 +70,7 @@
     eg_recv,
     cp,
     cp_recv,
+    srow,
     sm,
     sb,
     sp,
@@ -78,9 +79,9 @@
     qe,
     qe_recv,
     gi,
-    gd,
     gw,
-    sd,
+    src,
+    fp,
     fr,
     x3,
     x3e,
@@ -109,6 +110,10 @@
     air = g == 0
     has = {-1: i > 0, 0: None, 1: i < lats - 1}
 
+    def run(steps, body):
+        for step in steps:
+            body(step, 0)
+
     def place(group, di, dj):
         return (group, i + di, lax.rem(j + dj + lons, lons))
 
@@ -123,6 +128,9 @@
     low = sub8 < 4
     lane80 = iota((CH, LANES), 1)
     lane16 = iota((16, LANES), 1)
+    inner8 = lane8 & 15
+    air_shift = jnp.where(air, 2, 0)
+    ocean_shift = jnp.where(ocean, 2, 0)
 
     pairs = (
         (state_hbm, state_ref),
@@ -153,14 +161,14 @@
         for load in loads[5:8]:
             load.start()
 
+    q[...] = jnp.zeros((24, 8, LANES), F32)
     for di, block, rows in ((-1, 0, slice(0, 2)), (1, 2, slice(18, 20))):
         def blank(block=block, rows=rows):
             for s in range(STEPS):
                 xr[s, rows] = jnp.zeros((2, CH, LANES), BF)
-                sb[s, slice(0, 48) if block == 0 else slice(112, 160)] = jnp.zeros((48, LANES), BF)
+                sb[s, slice(0, 2) if block == 0 else slice(5, 7)] = jnp.zeros((2, 32, LANES), BF)
                 sp_recv[s, block] = jnp.zeros((2, 16, LANES), BF)
                 cp_recv[s, block // 2] = jnp.zeros((2, 16, LANES), BF)
-            q[rows] = jnp.zeros((2, 8, LANES), F32)
             qe_recv[block] = jnp.zeros((2, 8, LANES), F32)
 
         pl.when(jnp.logical_not(has[di]))(blank)
@@ -196,15 +204,19 @@
             device_id_type=MESH,
         )
 
-    def s_copy(s, di, dj):
+    def s_copy(s, wide, di, dj):
         n = 1 - di
         if dj == 0:
-            src = {0: sm.at[s], 1: sm.at[s, pl.ds(16, 48)], -1: sm.at[s, pl.ds(0, 48)]}[di]
-            dst = sb.at[s, pl.ds(48, 64)] if di == 0 else sb.at[s, pl.ds(0 if di == 1 else 112, 48)]
+            first = 1 if di == 1 else 0
+            count = (3 if di == 0 else 2) if wide else (2 if di == 0 else 1)
+            source = sm.at[s, pl.ds(first, count)]
+            target = sb.at[s, pl.ds({1: 0, 0: 2, -1: 5}[di], count)]
         else:
-            src = sp.at[s]
-            dst = sp_recv.at[s, n, 0 if dj == 1 else 1]
-        return remote(src, dst, s_send.at[s, n, dj + 1], s_recv.at[s, n, dj + 1], place(1 - g, di, dj))
+            source = sp.at[s, 0 if dj == -1 else 1]
+            target = sp_recv.at[s, n, 0 if dj == 1 else 1]
+        return remote(
+            source, target, s_send.at[s, n, dj + 1], s_recv.at[s, n, dj + 1], place(1 - g, di, dj)
+        )
 
     def x_copy(s, di, dj):
         n = 1 - di
@@ -232,6 +244,15 @@
     around = [(di, dj) for di in (-1, 0, 1) for dj in (-1, 0, 1)]
     ring = [(di, dj) for di, dj in around if di or dj]
 
+    def s_all(action, s, sending):
+        @pl.when(air)
+        def _():
+            action(functools.partial(s_copy, s, sending), around)
+
+        @pl.when(ocean)
+        def _():
+            action(functools.partial(s_copy, s, not sending), around)
+
     def start_all(make, pairs):
         for di, dj in pairs:
             when(has[di], lambda di=di, dj=dj: make(di, dj).start())
@@ -251,53 +272,79 @@
         xr[0, r + 2] = flip[pl.ds(r, CH, stride=ROWS), :].astype(BF)
         return c
 
-    lax.fori_loop(0, ROWS, to_rows, 0, unroll=4)
+    run(range(ROWS), to_rows)
 
     loads[1].wait()
     loads[4].wait()
     wet_values = mask_ref[...].astype(F32)
     wet[...] = wet_values
     kept = jnp.where(ocean, wet_values, 1.0)
-    for pair in range(ROWS // 2):
-        upper = jnp.broadcast_to(kept[2 * pair : 2 * pair + 1], (8, LANES))
-        lower = jnp.broadcast_to(kept[2 * pair + 1 : 2 * pair + 2], (8, LANES))
-        keep[8 * pair : 8 * pair + 8] = jnp.where(low, upper, lower)
+    keep[...] = kept
     high, middle, rest = thirds(proj_ref[g])
     pp[...] = jnp.concatenate([high, high, middle, middle, rest, rest], 0).astype(BF)
 
+    srow[...] = jnp.zeros((24, 8, LANES), F32)
+    def blocks_swapped(tiles):
+        tiles = list(tiles)
+        block = iota(tiles[0].shape, 1) >> 4
+        for s in (4, 2, 1):
+            stays = (block & s) == 0
+            for a in range(8):
+                if not a & s:
+                    x, y = tiles[a], tiles[a + s]
+                    tiles[a] = jnp.where(stays, x, pltpu.roll(y, 16 * s, 1))
+                    tiles[a + s] = jnp.where(stays, pltpu.roll(x, LANES - 16 * s, 1), y)
+        return tiles
+
+    def turned(x):
+        return pltpu.roll(x, 4, 0)
+
+    def double_low(x):
+        return jnp.where(low, x, turned(x))
+
+    def double_high(x):
+        return jnp.where(low, turned(x), x)
+
     def surface(s):
-        def four(m, c):
-            t = 4 * m + 2
-            rows = jnp.concatenate([xr[s, t + u] for u in range(4)], 1)
+        for m in range(4):
+            rows = jnp.concatenate([xr[s, 4 * m + 2 + u] for u in range(4)], 1)
             parts = jnp.dot(pp[...], rows, preferred_element_type=F32)
             fields = parts[0:8] + parts[8:16] + parts[16:24]
-            pairs = [
-                jnp.where(
-                    low,
-                    fields[:, 256 * u : 256 * u + 128],
-                    fields[:, 256 * u + 128 : 256 * u + 256],
-                )
-                for u in range(2)
-            ]
-            start = pl.multiple_of(16 * m, 16)
-            both = jnp.concatenate(pairs, 0) * keep[pl.ds(start, 16), :]
-            sm[s, pl.ds(start, 16), :] = both.astype(BF)
-            return c
-
-        lax.fori_loop(0, 4, four, 0, unroll=True)
-        packed = jnp.zeros((16, LANES), F32)
-        slot = ((lane16 + 16) >> 5) & 3
-        for m in range(4):
-            tile = sm[s, 16 * m : 16 * m + 16].astype(F32)
-            packed = jnp.where(slot == m, pltpu.roll(tile, 32 * m, 1) if m else tile, packed)
-        sp[s] = packed.astype(BF)
-
-    def edges(s):
+            for u in range(4):
+                r = 4 * m + u
+                kept_row = jnp.broadcast_to(keep[r : r + 1], (8, LANES))
+                srow[air_shift + r] = fields[:, 128 * u : 128 * u + 128] * kept_row
+        zero = jnp.zeros((8, LANES), F32)
+        tiles = blocks_swapped(
+            jnp.concatenate(
+                [jnp.where(low, srow[k], srow[8 + k]), jnp.where(low, srow[16 + k], zero)], 0
+            ).astype(BF)
+            for k in range(8)
+        )
+        sp[s, 0] = tiles[0]
+        sp[s, 1] = tiles[7]
+        tiles = [tile.astype(F32) for tile in tiles]
+        for half in range(2):
+            made = [[], [], []]
+            for m in range(2):
+                even, odd = tiles[4 * half + 2 * m], tiles[4 * half + 2 * m + 1]
+                made[0].append(jnp.where(low, even[0:8], turned(odd[0:8])))
+                made[1].append(jnp.where(low, turned(even[0:8]), odd[0:8]))
+                made[2].append(jnp.where(low, even[8:16], turned(odd[8:16])))
+            for band in range(3):
+                sm[s, band, 16 * half : 16 * half + 16] = jnp.concatenate(made[band], 0).astype(BF)
+
+    def edge_rows(s):
         def add(t, acc):
             return jnp.where((lane80 >> 2) == t, pltpu.roll(xr[s, t], 4 * t + 2, 1), acc)
 
-        own = lax.fori_loop(2, 18, add, jnp.zeros((CH, LANES), BF), unroll=4)
+        own = jnp.zeros((CH, LANES), BF)
+        for t in range(2, 18):
+            own = add(t, own)
         eg[s] = own
+
+    def corner_rows(s):
+        own = eg[s]
         packed = jnp.zeros((16, LANES), BF)
         for part in range(5):
             tile = pltpu.roll(own[16 * part : 16 * part + 16], 64 + 8 * part, 1)
@@ -315,26 +362,31 @@
         flip[16 * k : 16 * k + 16] = code.astype(F32)
         flip[64 + 16 * k : 64 + 16 * k + 16] = weights_ref[0, k]
     for r in range(ROWS):
-        q[r + 2] = flip[pl.ds(r, 8, stride=ROWS), :]
+        q[ocean_shift + r] = flip[pl.ds(r, 8, stride=ROWS), :]
 
     @pl.when(ocean)
     def _():
-        edges(0)
+        edge_rows(0)
+        corner_rows(0)
+        eg[1] = jnp.zeros((CH, LANES), BF)
 
         def add(t, acc):
             return jnp.where((lane8 >> 2) == t, pltpu.roll(q[t], 4 * t + 2, 1), acc)
 
-        qe[...] = lax.fori_loop(2, 18, add, jnp.zeros((8, LANES), F32))
+        own = jnp.zeros((8, LANES), F32)
+        for t in range(2, 18):
+            own = add(t, own)
+        qe[...] = own
 
     neighbours = 1 + has[-1].astype(I32) + has[1].astype(I32)
     pl.semaphore_wait(barrier, 3 * neighbours + g * (3 * neighbours - 1))
 
-    start_all(functools.partial(s_copy, 0), around)
+    s_all(start_all, 0, True)
 
     @pl.when(ocean)
     def _():
+        start_all(q_copy, ring)
         start_all(functools.partial(x_copy, 0), ring)
-        start_all(q_copy, ring)
 
     @pl.when(ocean)
     def _():
@@ -370,99 +422,153 @@
         )
         wa[...] = stacked.T[:, 0:96].astype(BF)
 
-    def decode(values, t, column, row):
-        for kp in range(2):
-            def spread(base):
-                first = jnp.broadcast_to(values[base + 2 * kp : base + 2 * kp + 1], (8, LANES))
-                second = jnp.broadcast_to(values[base + 2 * kp + 1 : base + 2 * kp + 2], (8, LANES))
-                return jnp.where(low, first, second)
-
-            code = spread(0).astype(I32)
-            source = column + (code & 31) - HW
-            inside = (source >= 0) & (source < LANES)
-            gi[t, kp] = (source & (LANES - 1)) + jnp.where(inside, 0, LANES)
-            gd[t, kp] = (code >> 5) + row
-            gw[t, kp] = spread(4)
-
-    def decode_row(t, c):
-        decode(q[t], t, lane8, 0)
-        return c
-
-    lax.fori_loop(2, 18, decode_row, 0, unroll=2)
+    def spread(values, base):
+        first = jnp.broadcast_to(values[base : base + 1], (8, LANES))
+        second = jnp.broadcast_to(values[base + 1 : base + 2], (8, LANES))
+        return jnp.where(low, first, second)
+
+    def decode_band(band):
+        tiles = blocks_swapped(q[8 * band + k] for k in range(8))
+        for patch in range(8):
+            for kp in range(2):
+                code = spread(tiles[patch], 2 * kp).astype(I32)
+                down = (lane8 >> 4) + (code >> 5)
+                across = inner8 + (code & 31)
+                beside = jnp.where((across >= 8) & (across < 24), 0, 1)
+                gi[8 * band + patch, kp] = (
+                    ((down & 7) * 16 + ((across + 8) & 15)) + ((down >> 3) * 2 + beside) * LANES
+                )
+                gw[8 * band + patch, kp] = spread(tiles[patch], 4 + 2 * kp)
+
+    @pl.when(air)
+    def _():
+        decode_band(0)
+        decode_band(1)
 
     @pl.when(ocean)
     def _():
+        decode_band(1)
         wait_arrivals(q_copy, ring)
-        lax.fori_loop(0, 2, decode_row, 0)
-        lax.fori_loop(18, 20, decode_row, 0)
+        decode_band(0)
+        decode_band(2)
         pos = lane8 & 3
         beside = [jnp.where(pos < 2, qe_recv[n, 0], qe_recv[n, 1]) for n in range(3)]
         ends = jnp.where(
             lane8 < 64, pltpu.roll(beside[0], 64, 1), pltpu.roll(beside[2], 64, 1)
         )
         values = jnp.where((lane8 >= 8) & (lane8 < 72), beside[1], ends)
-        decode(values, TALL, jnp.where(pos < 2, pos - 2, pos + 126), lane8 >> 2)
-
-    def spread_pair(row, which, values):
-        turned = pltpu.roll(values, 4, 0)
-        sd[row, which] = jnp.where(low, values, turned)
-        sd[row + 1, which] = jnp.where(low, turned, values)
+        for kp in range(2):
+            code = spread(values, 2 * kp).astype(I32)
+            down = (lane8 >> 2) + (code >> 5)
+            across = jnp.where(pos < 2, pos - 2, pos + 126) + (code & 31) - HW
+            outer = jnp.where((across >= 0) & (across < LANES), 0, 1)
+            gi[24, kp] = ((down & 7) * 16 + (across & 15)) + ((down >> 3) * 2 + outer) * LANES
+            gw[24, kp] = spread(values, 4 + 2 * kp)
+
+    def put_band(s, row, pick):
+        for quarter in range(2):
+            tile = pick(slice(16 * quarter, 16 * quarter + 16))
+            for m in range(2):
+                values = tile[8 * m : 8 * m + 8]
+                src[row, 4 * quarter + 2 * m + 1] = double_low(values)
+                src[row, 4 * quarter + 2 * m + 2] = double_high(values)
 
     def sources(s):
-        def main(m, c):
-            tile = sb[s, pl.ds(pl.multiple_of(16 * m, 16), 16), :].astype(F32)
-            spread_pair(4 * m, 0, tile[0:8])
-            spread_pair(4 * m + 2, 0, tile[8:16])
-            return c
-
-        lax.fori_loop(0, 10, main, 0, unroll=2)
-        right = ((lane16 + 16) & 31) >= 16
-        for n in range(3):
-            tile = jnp.where(right, sp_recv[s, n, 1].astype(F32), sp_recv[s, n, 0].astype(F32))
-            for m in range(4):
-                row = 16 * n + 4 * m - 4
-                if 0 <= row < 40:
-                    turned = pltpu.roll(tile, LANES - 32 * m, 1) if m else tile
-                    spread_pair(row, 1, turned[0:8])
-                    spread_pair(row + 2, 1, turned[8:16])
+        def band(k):
+            return lambda rows: sb[s, k, rows].astype(F32)
+
+        def joined(k):
+            return lambda rows: jnp.where(
+                lane16 < 32, sb[s, k, rows].astype(F32), sb[s, k + 1, rows].astype(F32)
+            )
+
+        sides = [[sp_recv[s, n, side].astype(F32) for side in range(2)] for n in range(3)]
+
+        @pl.when(air)
+        def _():
+            for row, k in enumerate((0, 2, 3, 5)):
+                put_band(s, row, band(k))
+            for side in range(2):
+                north, center, south = (sides[n][side] for n in range(3))
+                column = 9 * side
+                src[0, column] = double_high(north[0:8])
+                src[1, column] = double_low(center[0:8])
+                src[2, column] = double_high(center[0:8])
+                src[3, column] = double_low(south[0:8])
+
+        @pl.when(ocean)
+        def _():
+            for row, pick in enumerate((band(0), joined(1), band(3), joined(4), band(6))):
+                put_band(s, row, pick)
+            first = lane8 < 32
+            for side in range(2):
+                north, center, south = (sides[n][side] for n in range(3))
+                column = 9 * side
+                src[0, column] = double_high(north[0:8])
+                src[1, column] = jnp.where(first, double_low(north[8:16]), double_low(center[0:8]))
+                src[2, column] = double_high(center[0:8])
+                src[3, column] = jnp.where(first, double_low(center[8:16]), double_low(south[0:8]))
+                src[4, column] = double_high(south[0:8])
 
     def take(values, index):
         return jnp.take_along_axis(values, index, axis=1, mode="promise_in_bounds")
 
-    def combine(t, picked):
-        total = picked[0] * gw[t, 0] + picked[1] * gw[t, 1]
-        return total + pltpu.roll(total, 4, 0)
-
-    def regrid_row(t, c):
-        index = [gi[t, kp] & (LANES - 1) for kp in range(2)]
-        beyond = [gi[t, kp] >= LANES for kp in range(2)]
-        depth = [gd[t, kp] for kp in range(2)]
-        picked = [jnp.zeros((8, LANES), F32) for kp in range(2)]
-        for d in range(2 * HW + 1):
-            here = sd[t + d + 2, 0]
-            there = sd[t + d + 2, 1]
-            for kp in range(2):
-                value = jnp.where(beyond[kp], take(there, index[kp]), take(here, index[kp]))
-                picked[kp] = jnp.where(depth[kp] == d, value, picked[kp])
-        fr[t] = combine(t, picked)
+    def combine(n, picked):
+        total = picked[0] * gw[n, 0] + picked[1] * gw[n, 1]
+        return total + turned(total)
+
+    def regrid_patch(n, c):
+        band = n >> 3
+        patch = n & 7
+        picked = []
+        here = [src[band + d, patch + 1] for d in range(3)]
+        there = [
+            jnp.where(inner8 < 8, src[band + d, patch + 2], src[band + d, patch]) for d in range(3)
+        ]
+        for kp in range(2):
+            index = gi[n, kp] & (LANES - 1)
+            which = gi[n, kp] >> 7
+            value = jnp.zeros((8, LANES), F32)
+            for d in range(3):
+                value = jnp.where(which == 2 * d, take(here[d], index), value)
+                value = jnp.where(which == 2 * d + 1, take(there[d], index), value)
+            picked.append(value)
+        fp[n] = combine(n, picked)
         return c
 
     def regrid_edges():
-        index = [gi[TALL, kp] & (LANES - 1) for kp in range(2)]
-        beyond = [gi[TALL, kp] >= LANES for kp in range(2)]
-        depth = [gd[TALL, kp] for kp in range(2)]
-
-        def body(d, picked):
-            here = sd[d + 2, 0]
-            there = sd[d + 2, 1]
-            out = []
-            for kp in range(2):
-                value = jnp.where(beyond[kp], take(there, index[kp]), take(here, index[kp]))
-                out.append(jnp.where(depth[kp] == d, value, picked[kp]))
-            return tuple(out)
-
+        picked = []
+        left = (lane8 & 3) < 2
+        for kp in range(2):
+            index = gi[24, kp] & (LANES - 1)
+            which = gi[24, kp] >> 7
+            value = jnp.zeros((8, LANES), F32)
+            for d in range(5):
+                inner = take(jnp.where(inner8 < 8, src[d, 1], src[d, 8]), index)
+                outer = jnp.where(left, take(src[d, 0], index), take(src[d, 9], index))
+                value = jnp.where(which == 2 * d, inner, value)
+                value = jnp.where(which == 2 * d + 1, outer, value)
+            picked.append(value)
+        fp[24] = combine(24, picked)
+
+    def forcing_rows(bands):
         zero = jnp.zeros((8, LANES), F32)
-        fr[TALL] = combine(TALL, lax.fori_loop(0, TALL + 2 * HW, body, (zero, zero), unroll=4))
+        tiles = blocks_swapped(
+            jnp.concatenate(
+                [
+                    jnp.where(low, fp[k], fp[8 + k]),
+                    jnp.where(low, fp[16 + k], zero) if bands == 3 else zero,
+                ],
+                0,
+            ).astype(BF)
+            for k in range(8)
+        )
+        for k in range(8):
+            tile = tiles[k].astype(F32)
+            fr[k] = double_low(tile[0:8])
+            fr[8 + k] = double_high(tile[0:8])
+            if bands == 3 and k < 4:
+                fr[16 + k] = double_low(tile[8:16])
 
     def finish_row(s, r, values):
         if s + 1 < STEPS:
@@ -471,7 +577,8 @@
             flip[pl.ds(r, CH, stride=ROWS), :] = values
 
     def air_step(s):
-        lax.fori_loop(2, 18, regrid_row, 0)
+        run(range(16), regrid_patch)
+        forcing_rows(2)
         ones = jnp.where(sub8 < 7, 1.0, 0.0)
         blank = jnp.zeros((8, LANES), F32)
 
@@ -479,7 +586,7 @@
             t = 2 * p + 2
             columns = []
             for u in range(2):
-                tail = jnp.concatenate([jnp.where(low, fr[t + u], ones), blank], 0).astype(BF)
+                tail = jnp.concatenate([jnp.where(low, fr[t + u - 2], ones), blank], 0).astype(BF)
                 columns.append(jnp.concatenate([xr[s, t + u], tail], 0))
             hidden = gelu(
                 jnp.dot(wa[...], jnp.concatenate(columns, 1), preferred_element_type=F32)
@@ -490,11 +597,12 @@
                 finish_row(s, 2 * p + u, new)
             return c
 
-        lax.fori_loop(0, ROWS // 2, pair, 0)
+        run(range(ROWS // 2), pair)
 
     def ocean_step(s):
-        lax.fori_loop(0, TALL, regrid_row, 0)
+        run(range(24), regrid_patch)
         regrid_edges()
+        forcing_rows(3)
         wait_arrivals(functools.partial(x_copy, s), ring)
 
         pos = lane80 & 3
@@ -529,8 +637,10 @@
         def add(t, acc):
             return jnp.where((lane8 >> 2) == t, pltpu.roll(fr[t], 4 * t + 2, 1), acc)
 
-        own_forcing = lax.fori_loop(0, TALL, add, jnp.zeros((8, LANES), F32), unroll=4)
-        beside_forcing = fr[TALL]
+        own_forcing = jnp.zeros((8, LANES), F32)
+        for t in range(TALL):
+            own_forcing = add(t, own_forcing)
+        beside_forcing = fp[24]
         first, second, third = taps(beside_forcing, own_forcing, pos8)
         ones = jnp.where(sub8 < 7, 1.0, 0.0)
         x3e[240:256] = jnp.concatenate(
@@ -540,22 +650,21 @@
 
         def widen(t, c):
             forcing = fr[t]
-            turned = pltpu.roll(swapped_forcing, 126 - 4 * t, 1)
-            left = jnp.where(lane8 == 0, turned, pltpu.roll(forcing, 1, 1))
-            right = jnp.where(lane8 == LANES - 1, turned, pltpu.roll(forcing, LANES - 1, 1))
+            halo = pltpu.roll(swapped_forcing, 126 - 4 * t, 1)
+            left = jnp.where(lane8 == 0, halo, pltpu.roll(forcing, 1, 1))
+            right = jnp.where(lane8 == LANES - 1, halo, pltpu.roll(forcing, LANES - 1, 1))
             x3[t, 240:256] = jnp.concatenate(
                 [jnp.where(low, left, forcing), jnp.where(low, right, ones)], 0
             ).astype(BF)
             cells = xr[s, t]
-            turned = pltpu.roll(hh[...], 126 - 4 * t, 1)
-            x3[t, 0:80] = jnp.where(lane80 == 0, turned, pltpu.roll(cells, 1, 1))
+            halo = pltpu.roll(hh[...], 126 - 4 * t, 1)
+            x3[t, 0:80] = jnp.where(lane80 == 0, halo, pltpu.roll(cells, 1, 1))
             x3[t, 80:160] = cells
             x3[t, 160:240] = jnp.where(
-                lane80 == LANES - 1, turned, pltpu.roll(cells, LANES - 1, 1)
+                lane80 == LANES - 1, halo, pltpu.roll(cells, LANES - 1, 1)
             )
-            return c
-
-        lax.fori_loop(0, TALL, widen, 0, unroll=2)
+
+        run(range(TALL), widen)
 
         def first_conv(p, c):
             h = 2 * p
@@ -568,7 +677,7 @@
             hid[h + 1] = active[:, 128:256]
             return c
 
-        lax.fori_loop(0, 9, first_conv, 0)
+        run(range(9), first_conv)
 
         @pl.when(i == 0)
         def _():
@@ -607,29 +716,37 @@
                 total = total + jnp.dot(w2[a], columns, preferred_element_type=F32)
             for u in range(2):
                 part = total[:, 128 * u : 128 * u + 128]
-                turned = pltpu.roll(ze[...], 126 - 4 * (r + u), 1)
-                left = jnp.where(lane80 == 0, turned, pltpu.roll(part[0:80], 1, 1))
+                halo = pltpu.roll(ze[...], 126 - 4 * (r + u), 1)
+                left = jnp.where(lane80 == 0, halo, pltpu.roll(part[0:80], 1, 1))
                 right = jnp.where(
-                    lane80 == LANES - 1, turned, pltpu.roll(part[160:240], LANES - 1, 1)
+                    lane80 == LANES - 1, halo, pltpu.roll(part[160:240], LANES - 1, 1)
                 )
                 update = left + part[80:160] + right
-                new = xr[s, r + u + 2].astype(F32) + wet[pl.ds(r + u, 1), :] * update
+                new = xr[s, r + u + 2].astype(F32) + wet[r + u : r + u + 1] * update
                 finish_row(s, r + u, new)
+                if s + 1 < STEPS:
+                    t = r + u + 2
+                    eg[s + 1] = jnp.where(
+                        (lane80 >> 2) == t, pltpu.roll(new.astype(BF), 4 * t + 2, 1), eg[s + 1]
+                    )
             return c
 
-        lax.fori_loop(0, ROWS // 2, second_conv, 0)
+        run((0, 7), second_conv)
+        if s + 1 < STEPS:
+            start_all(functools.partial(x_copy, s + 1), [(-1, 0), (1, 0)])
+        run(range(1, 7), second_conv)
+        if s + 1 < STEPS:
+            corner_rows(s + 1)
+            start_all(
+                functools.partial(x_copy, s + 1), [(di, dj) for di, dj in ring if dj]
+            )
 
     for s in range(STEPS):
         if s:
             surface(s)
-            start_all(functools.partial(s_copy, s), around)
-
-            @pl.when(ocean)
-            def _(s=s):
-                edges(s)
-                start_all(functools.partial(x_copy, s), ring)
-
-        wait_arrivals(functools.partial(s_copy, s), around)
+            s_all(start_all, s, True)
+
+        s_all(wait_arrivals, s, False)
         sources(s)
 
         @pl.when(ocean)
@@ -643,7 +760,7 @@
     out_ref[0] = flip[...].reshape(CH, ROWS, LANES).astype(BF)
 
     for s in range(STEPS):
-        wait_departures(functools.partial(s_copy, s), around)
+        s_all(wait_departures, s, True)
 
     @pl.when(ocean)
     def _():
@@ -686,18 +803,19 @@
                 pltpu.VMEM((STEPS, 2, CH, LANES), BF),
                 pltpu.VMEM((STEPS, 16, LANES), BF),
                 pltpu.VMEM((STEPS, 2, 2, 16, LANES), BF),
-                pltpu.VMEM((STEPS, 64, LANES), BF),
-                pltpu.VMEM((STEPS, 160, LANES), BF),
-                pltpu.VMEM((STEPS, 16, LANES), BF),
+                pltpu.VMEM((24, 8, LANES), F32),
+                pltpu.VMEM((STEPS, 3, 32, LANES), BF),
+                pltpu.VMEM((STEPS, 7, 32, LANES), BF),
+                pltpu.VMEM((STEPS, 2, 16, LANES), BF),
                 pltpu.VMEM((STEPS, 3, 2, 16, LANES), BF),
-                pltpu.VMEM((TALL, 8, LANES), F32),
+                pltpu.VMEM((24, 8, LANES), F32),
                 pltpu.VMEM((8, LANES), F32),
                 pltpu.VMEM((3, 2, 8, LANES), F32),
-                pltpu.VMEM((TALL + 1, 2, 8, LANES), I32),
-                pltpu.VMEM((TALL + 1, 2, 8, LANES), I32),
-                pltpu.VMEM((TALL + 1, 2, 8, LANES), F32),
-                pltpu.VMEM((40, 2, 8, LANES), F32),
-                pltpu.VMEM((TALL + 1, 8, LANES), F32),
+                pltpu.VMEM((25, 2, 8, LANES), I32),
+                pltpu.VMEM((25, 2, 8, LANES), F32),
+                pltpu.VMEM((5, 10, 8, LANES), F32),
+                pltpu.VMEM((25, 8, LANES), F32),
+                pltpu.VMEM((24, 8, LANES), F32),
                 pltpu.VMEM((TALL, 256, LANES), BF),
                 pltpu.VMEM((256, LANES), BF),
                 pltpu.VMEM((3, HOP, 256), BF),
@@ -707,7 +825,7 @@
                 pltpu.VMEM((HOP, LANES), BF),
                 pltpu.VMEM((CH, LANES), BF),
                 pltpu.VMEM((CH, LANES), F32),
-                pltpu.VMEM((64, LANES), F32),
+                pltpu.VMEM((ROWS, LANES), F32),
                 pltpu.VMEM((ROWS, LANES), F32),
                 pltpu.VMEM((24, CH), BF),
                 dma((11,)),

time: 43.2 us -> 27 us (0.62)
  Pallas kernels: 41.4 us -> 25.2 us
    pallas_call x1, Pallas kernels: 41.4 us -> 25.2 us  [local(): pl.pallas_call(functools.partial(kernel, lats, lons), out_shape=jax.Shape...]
where the time goes in v3:
time: 27 us; the launch traced here: 26.9 us
  Pallas kernels  25.2 us (93%)
  local copies, waits for them, and re-layouts  1.72 us (6%)
    pallas_call x1, Pallas kernels, local(): pl.pallas_call(functools.partial(kernel, lats, lons), out_shape=jax.Shape...  25.2 us
    unnamed x1, local copies, waits for them, and re-layouts  1.72 us

profile of v3, /device:TPU:102, one launch (start us, length us, event | category | flops | bytes accessed | tf_op | source)
XLA Modules:
  0.0 26.9 jit_solution(8811398414965102575)
XLA Ops:
  0.0 25.2 %shard_map.109 = bf16[1,80,16,128]{3,2,1,0:T(8,128)(2,1)} custom-call(bf16[1,80,16,128]{3,2,1,0:T(8,128)(2,1)} %state_hbm.1, s32[16,128]{1,0:T(8,128)} %mask_hbm.1, s32[1,2,4,16,128]{4,3,2,1,0:T(8,128)} %offsets_hbm.1, f32[1,4,16,128]{3,2,1,0:T(8,128)} %weights_hbm.1, f32[2,4,80]{2,1,0:T(4,128)} %proj_hbm.1, bf16[84,384]{1,0:T(8,128)(2,1)} %bitcast.5, ...), custom_call_target="tpu_custom_call" | custom-call | tf_op jit(solution)/shard_map/pallas_call | solution.py:783
  25.2 1.7 %copy.13 = bf16[1,80,16,128]{3,2,1,0:T(8,128)(2,1)} copy(bf16[1,80,16,128]{3,2,1,0:T(8,128)(2,1)} %shard_map.109) | data formatting | bytes 655360

commit v4 on v3

--- a/solution.py
+++ b/solution.py
@@ -20,15 +20,16 @@
 ROWS = 16
 LANES = 128
 TALL = ROWS + 4
+AIR_ROWS = 16
+SURFACE_ROWS = 4
 
 
 def iota(shape, axis):
     return lax.broadcasted_iota(I32, shape, axis)
 
 
-def gelu(x):
-    inner = x * (0.7978845608028654 + 0.035677408136300125 * (x * x))
-    half = 0.5 * x
+def gelu_of_twice(half):
+    inner = half * (1.5957691216057308 + 0.285419265090401 * (half * half))
     return half + half * jnp.tanh(inner)
 
 
@@ -65,6 +66,7 @@
     ocn_bias_ref,
     ocn_out_v,
     flip,
+    final,
     xr,
     eg,
     eg_recv,
@@ -81,6 +83,7 @@
     gi,
     gw,
     src,
+    part,
     fp,
     fr,
     x3,
@@ -241,7 +244,7 @@
             dst = qe_recv.at[n, 0 if dj == 1 else 1]
         return remote(src, dst, q_send.at[n, dj + 1], q_recv.at[n, dj + 1], place(1, di, dj))
 
-    around = [(di, dj) for di in (-1, 0, 1) for dj in (-1, 0, 1)]
+    around = [(di, dj) for di in (-1, 1, 0) for dj in (-1, 1, 0)]
     ring = [(di, dj) for di, dj in around if di or dj]
 
     def s_all(action, s, sending):
@@ -266,13 +269,7 @@
             when(has[di], lambda di=di, dj=dj: make(di, dj).wait_send())
 
     loads[0].wait()
-    flip[...] = state_ref[0].astype(F32).reshape(CH * ROWS, LANES)
-
-    def to_rows(r, c):
-        xr[0, r + 2] = flip[pl.ds(r, CH, stride=ROWS), :].astype(BF)
-        return c
-
-    run(range(ROWS), to_rows)
+    xr[0, 2:18] = jnp.transpose(state_ref[0], (1, 0, 2))
 
     loads[1].wait()
     loads[4].wait()
@@ -305,15 +302,21 @@
     def double_high(x):
         return jnp.where(low, turned(x), x)
 
+    def fill(t, cells):
+        x3[t, 0:80] = pltpu.roll(cells, 1, 1)
+        x3[t, 80:160] = cells
+        x3[t, 160:240] = pltpu.roll(cells, LANES - 1, 1)
+
+    def surface_rows(first, rows):
+        parts = jnp.dot(pp[...], jnp.concatenate(rows, 1), preferred_element_type=F32)
+        fields = parts[0:8] + parts[8:16] + parts[16:24]
+        for u in range(len(rows)):
+            kept_row = jnp.broadcast_to(keep[first + u : first + u + 1], (8, LANES))
+            srow[air_shift + first + u] = fields[:, 128 * u : 128 * u + 128] * kept_row
+
     def surface(s):
-        for m in range(4):
-            rows = jnp.concatenate([xr[s, 4 * m + 2 + u] for u in range(4)], 1)
-            parts = jnp.dot(pp[...], rows, preferred_element_type=F32)
-            fields = parts[0:8] + parts[8:16] + parts[16:24]
-            for u in range(4):
-                r = 4 * m + u
-                kept_row = jnp.broadcast_to(keep[r : r + 1], (8, LANES))
-                srow[air_shift + r] = fields[:, 128 * u : 128 * u + 128] * kept_row
+        for m in range(0, ROWS, SURFACE_ROWS):
+            surface_rows(m, [xr[s, m + 2 + u] for u in range(SURFACE_ROWS)])
         zero = jnp.zeros((8, LANES), F32)
         tiles = blocks_swapped(
             jnp.concatenate(
@@ -387,6 +390,8 @@
     def _():
         start_all(q_copy, ring)
         start_all(functools.partial(x_copy, 0), ring)
+        for t in range(2, 18):
+            fill(t, xr[0, t])
 
     @pl.when(ocean)
     def _():
@@ -394,12 +399,12 @@
             load.wait()
 
         def rows_of(values):
-            return thirds(values.reshape(1, -1))
+            return thirds(0.5 * values.reshape(1, -1))
 
         spare = jnp.zeros((1, HO), F32)
         bias = jnp.concatenate([*rows_of(ocn_bias_ref[...]), spare], 0)
         for a in range(3):
-            taps = [ocn_in_v[3 * a + b].astype(F32) for b in range(3)]
+            taps = [0.5 * ocn_in_v[3 * a + b].astype(F32) for b in range(3)]
             last = bias if a == 1 else jnp.zeros((4, HO), F32)
             stacked = jnp.concatenate(
                 [tap[0:CH] for tap in taps] + [tap[CH:] for tap in taps] + [last], 0
@@ -416,9 +421,9 @@
     def _():
         for load in loads[5:8]:
             load.wait()
-        bias = thirds(atm_bias_ref[...].reshape(1, -1))
+        bias = thirds(0.5 * atm_bias_ref[...].reshape(1, -1))
         stacked = jnp.concatenate(
-            [atm_in_ref[...].astype(F32), *bias, jnp.zeros((41, 384), F32)], 0
+            [0.5 * atm_in_ref[...].astype(F32), *bias, jnp.zeros((41, 384), F32)], 0
         )
         wa[...] = stacked.T[:, 0:96].astype(BF)
 
@@ -465,6 +470,23 @@
             gi[24, kp] = ((down & 7) * 16 + (across & 15)) + ((down >> 3) * 2 + outer) * LANES
             gw[24, kp] = spread(values, 4 + 2 * kp)
 
+    def take(values, index):
+        return jnp.take_along_axis(values, index, axis=1, mode="promise_in_bounds")
+
+    def combine(n, picked):
+        total = picked[0] * gw[n, 0] + picked[1] * gw[n, 1]
+        return total + turned(total)
+
+    def gather(n, kp, value, steps):
+        band, patch = n >> 3, n & 7
+        index = gi[n, kp] & (LANES - 1)
+        which = gi[n, kp] >> 7
+        for d in steps:
+            there = jnp.where(inner8 < 8, src[band + d, patch + 2], src[band + d, patch])
+            value = jnp.where(which == 2 * d, take(src[band + d, patch + 1], index), value)
+            value = jnp.where(which == 2 * d + 1, take(there, index), value)
+        return value
+
     def put_band(s, row, pick):
         for quarter in range(2):
             tile = pick(slice(16 * quarter, 16 * quarter + 16))
@@ -482,22 +504,34 @@
                 lane16 < 32, sb[s, k, rows].astype(F32), sb[s, k + 1, rows].astype(F32)
             )
 
-        sides = [[sp_recv[s, n, side].astype(F32) for side in range(2)] for n in range(3)]
-
         @pl.when(air)
         def _():
-            for row, k in enumerate((0, 2, 3, 5)):
+            middle = [(0, dj) for dj in (-1, 1, 0)]
+            wait_arrivals(functools.partial(s_copy, s, False), middle)
+            sides = [[sp_recv[s, 1, side].astype(F32) for side in range(2)]]
+            for row, k in ((1, 2), (2, 3)):
                 put_band(s, row, band(k))
             for side in range(2):
-                north, center, south = (sides[n][side] for n in range(3))
-                column = 9 * side
-                src[0, column] = double_high(north[0:8])
-                src[1, column] = double_low(center[0:8])
-                src[2, column] = double_high(center[0:8])
-                src[3, column] = double_low(south[0:8])
+                src[1, 9 * side] = double_low(sides[0][side][0:8])
+                src[2, 9 * side] = double_high(sides[0][side][0:8])
+            blank = jnp.zeros((8, LANES), F32)
+            for n in range(16):
+                for kp in range(2):
+                    part[n, kp] = gather(n, kp, blank, (1, 2) if n < 8 else (0, 1))
+            beyond = [(di, dj) for di, dj in around if di]
+            wait_arrivals(functools.partial(s_copy, s, False), beyond)
+            for row, k, n, double in ((0, 0, 0, double_high), (3, 5, 2, double_low)):
+                put_band(s, row, band(k))
+                for side in range(2):
+                    src[row, 9 * side] = double(sp_recv[s, n, side].astype(F32)[0:8])
+            for n in range(16):
+                steps = (0,) if n < 8 else (2,)
+                fp[n] = combine(n, [gather(n, kp, part[n, kp], steps) for kp in range(2)])
 
         @pl.when(ocean)
         def _():
+            wait_arrivals(functools.partial(s_copy, s, True), around)
+            sides = [[sp_recv[s, n, side].astype(F32) for side in range(2)] for n in range(3)]
             for row, pick in enumerate((band(0), joined(1), band(3), joined(4), band(6))):
                 put_band(s, row, pick)
             first = lane8 < 32
@@ -510,31 +544,9 @@
                 src[3, column] = jnp.where(first, double_low(center[8:16]), double_low(south[0:8]))
                 src[4, column] = double_high(south[0:8])
 
-    def take(values, index):
-        return jnp.take_along_axis(values, index, axis=1, mode="promise_in_bounds")
-
-    def combine(n, picked):
-        total = picked[0] * gw[n, 0] + picked[1] * gw[n, 1]
-        return total + turned(total)
-
     def regrid_patch(n, c):
-        band = n >> 3
-        patch = n & 7
-        picked = []
-        here = [src[band + d, patch + 1] for d in range(3)]
-        there = [
-            jnp.where(inner8 < 8, src[band + d, patch + 2], src[band + d, patch]) for d in range(3)
-        ]
-        for kp in range(2):
-            index = gi[n, kp] & (LANES - 1)
-            which = gi[n, kp] >> 7
-            value = jnp.zeros((8, LANES), F32)
-            for d in range(3):
-                value = jnp.where(which == 2 * d, take(here[d], index), value)
-                value = jnp.where(which == 2 * d + 1, take(there[d], index), value)
-            picked.append(value)
-        fp[n] = combine(n, picked)
-        return c
+        blank = jnp.zeros((8, LANES), F32)
+        fp[n] = combine(n, [gather(n, kp, blank, range(3)) for kp in range(2)])
 
     def regrid_edges():
         picked = []
@@ -570,54 +582,46 @@
             if bands == 3 and k < 4:
                 fr[16 + k] = double_low(tile[8:16])
 
-    def finish_row(s, r, values):
-        if s + 1 < STEPS:
-            xr[s + 1, r + 2] = values.astype(BF)
-        else:
-            flip[pl.ds(r, CH, stride=ROWS), :] = values
+    def finish_rows(s, first, rows):
+        rows = [values.astype(BF) for values in rows]
+        for u, values in enumerate(rows):
+            if s + 1 < STEPS:
+                xr[s + 1, first + u + 2] = values
+            else:
+                final[first + u] = values
+        return rows
 
     def air_step(s):
-        run(range(16), regrid_patch)
         forcing_rows(2)
         ones = jnp.where(sub8 < 7, 1.0, 0.0)
         blank = jnp.zeros((8, LANES), F32)
 
-        def pair(p, c):
-            t = 2 * p + 2
-            columns = []
-            for u in range(2):
-                tail = jnp.concatenate([jnp.where(low, fr[t + u - 2], ones), blank], 0).astype(BF)
-                columns.append(jnp.concatenate([xr[s, t + u], tail], 0))
-            hidden = gelu(
-                jnp.dot(wa[...], jnp.concatenate(columns, 1), preferred_element_type=F32)
+        columns = []
+        for r in range(ROWS):
+            tail = jnp.concatenate([jnp.where(low, fr[r], ones), blank], 0).astype(BF)
+            columns.append(jnp.concatenate([xr[s, r + 2], tail], 0))
+        for first in range(0, ROWS, AIR_ROWS):
+            block = jnp.concatenate(columns[first : first + AIR_ROWS], 1)
+            hidden = gelu_of_twice(
+                jnp.dot(wa[...], block, preferred_element_type=F32)
             ).astype(BF)
             update = jnp.dot(atm_out_ref[...], hidden, preferred_element_type=F32)
-            for u in range(2):
-                new = xr[s, t + u].astype(F32) + update[:, 128 * u : 128 * u + 128]
-                finish_row(s, 2 * p + u, new)
-            return c
-
-        run(range(ROWS // 2), pair)
+            finish_rows(
+                s,
+                first,
+                [
+                    xr[s, first + u + 2].astype(F32) + update[:, 128 * u : 128 * u + 128]
+                    for u in range(AIR_ROWS)
+                ],
+            )
 
     def ocean_step(s):
         run(range(24), regrid_patch)
         regrid_edges()
         forcing_rows(3)
-        wait_arrivals(functools.partial(x_copy, s), ring)
-
         pos = lane80 & 3
         pos8 = lane8 & 3
-        own = eg[s]
-        for t in (0, 1, 18, 19):
-            own = jnp.where((lane80 >> 2) == t, pltpu.roll(xr[s, t], 4 * t + 2, 1), own)
-        beside = jnp.where(pos < 2, eg_recv[s, 0], eg_recv[s, 1])
         pos16 = lane16 & 3
-        corners = [jnp.where(pos16 < 2, cp_recv[s, n, 0], cp_recv[s, n, 1]) for n in range(2)]
-        corner = jnp.where(lane16 < 64, corners[0], corners[1])
-        corner = jnp.concatenate(
-            [pltpu.roll(corner, LANES - 8 * part, 1) if part else corner for part in range(5)], 0
-        )
-        beside = jnp.where((lane80 >= 8) & (lane80 < 72), beside, corner)
 
         def taps(halo, mine, where):
             return (
@@ -629,17 +633,9 @@
         def swapped(halo, where):
             return jnp.where(where == 1, pltpu.roll(halo, LANES - 1, 1), pltpu.roll(halo, 1, 1))
 
-        state_taps = taps(beside, own, pos)
-        for b in range(3):
-            x3e[CH * b : CH * b + CH] = state_taps[b]
-        hh[...] = swapped(beside, pos)
-
-        def add(t, acc):
-            return jnp.where((lane8 >> 2) == t, pltpu.roll(fr[t], 4 * t + 2, 1), acc)
-
         own_forcing = jnp.zeros((8, LANES), F32)
         for t in range(TALL):
-            own_forcing = add(t, own_forcing)
+            own_forcing = jnp.where((lane8 >> 2) == t, pltpu.roll(fr[t], 4 * t + 2, 1), own_forcing)
         beside_forcing = fp[24]
         first, second, third = taps(beside_forcing, own_forcing, pos8)
         ones = jnp.where(sub8 < 7, 1.0, 0.0)
@@ -647,8 +643,7 @@
             [jnp.where(low, first, second), jnp.where(low, third, ones)], 0
         ).astype(BF)
         swapped_forcing = swapped(beside_forcing, pos8)
-
-        def widen(t, c):
+        for t in range(TALL):
             forcing = fr[t]
             halo = pltpu.roll(swapped_forcing, 126 - 4 * t, 1)
             left = jnp.where(lane8 == 0, halo, pltpu.roll(forcing, 1, 1))
@@ -656,15 +651,11 @@
             x3[t, 240:256] = jnp.concatenate(
                 [jnp.where(low, left, forcing), jnp.where(low, right, ones)], 0
             ).astype(BF)
-            cells = xr[s, t]
+
+        def rim(t):
             halo = pltpu.roll(hh[...], 126 - 4 * t, 1)
-            x3[t, 0:80] = jnp.where(lane80 == 0, halo, pltpu.roll(cells, 1, 1))
-            x3[t, 80:160] = cells
-            x3[t, 160:240] = jnp.where(
-                lane80 == LANES - 1, halo, pltpu.roll(cells, LANES - 1, 1)
-            )
-
-        run(range(TALL), widen)
+            x3[t, 0:80] = jnp.where(lane80 == 0, halo, x3[t, 0:80])
+            x3[t, 160:240] = jnp.where(lane80 == LANES - 1, halo, x3[t, 160:240])
 
         def first_conv(p, c):
             h = 2 * p
@@ -672,20 +663,40 @@
             for a in range(3):
                 columns = jnp.concatenate([x3[h + a], x3[h + a + 1]], 1)
                 total = total + jnp.dot(w1[a], columns, preferred_element_type=F32)
-            active = gelu(total).astype(BF)
+            active = gelu_of_twice(total)
+            if p == 0:
+                active = jnp.where((iota((HOP, 256), 1) < 128) & (i == 0), 0.0, active)
+            if p == 8:
+                active = jnp.where((iota((HOP, 256), 1) >= 128) & (i == lats - 1), 0.0, active)
+            active = active.astype(BF)
             hid[h] = active[:, 0:128]
             hid[h + 1] = active[:, 128:256]
-            return c
-
-        run(range(9), first_conv)
-
-        @pl.when(i == 0)
-        def _():
-            hid[0] = jnp.zeros((HOP, LANES), BF)
-
-        @pl.when(i == lats - 1)
-        def _():
-            hid[17] = jnp.zeros((HOP, LANES), BF)
+
+        wait_arrivals(functools.partial(x_copy, s), [(0, -1), (0, 1)])
+        beside = jnp.where(pos < 2, eg_recv[s, 0], eg_recv[s, 1])
+        hh[...] = swapped(beside, pos)
+        for t in range(2, 18):
+            rim(t)
+        run(range(1, 8), first_conv)
+
+        wait_arrivals(functools.partial(x_copy, s), [(di, dj) for di, dj in ring if di])
+        own = eg[s]
+        for t in (0, 1, 18, 19):
+            own = jnp.where((lane80 >> 2) == t, pltpu.roll(xr[s, t], 4 * t + 2, 1), own)
+        ends = [jnp.where(pos16 < 2, cp_recv[s, n, 0], cp_recv[s, n, 1]) for n in range(2)]
+        corner = jnp.where(lane16 < 64, ends[0], ends[1])
+        corner = jnp.concatenate(
+            [pltpu.roll(corner, LANES - 8 * part, 1) if part else corner for part in range(5)], 0
+        )
+        beside = jnp.where((lane80 >= 8) & (lane80 < 72), beside, corner)
+        state_taps = taps(beside, own, pos)
+        for b in range(3):
+            x3e[CH * b : CH * b + CH] = state_taps[b]
+        hh[...] = swapped(beside, pos)
+        for t in (0, 1, 18, 19):
+            fill(t, xr[s, t])
+            rim(t)
+        run((0, 8), first_conv)
 
         total = jnp.zeros((HOP, LANES), F32)
         for a in range(3):
@@ -695,7 +706,7 @@
             total = total + jnp.dot(w1[a], columns, preferred_element_type=F32)
         slot = iota((HOP, LANES), 1) >> 2
         outside = ((slot == 0) & (i == 0)) | ((slot == 17) & (i == lats - 1))
-        he[...] = jnp.where(outside, 0.0, gelu(total)).astype(BF)
+        he[...] = jnp.where(outside, 0.0, gelu_of_twice(total)).astype(BF)
         total = jnp.zeros((240, LANES), F32)
         for a in range(3):
             columns = he[...]
@@ -714,6 +725,7 @@
             for a in range(3):
                 columns = jnp.concatenate([hid[r + a], hid[r + a + 1]], 1)
                 total = total + jnp.dot(w2[a], columns, preferred_element_type=F32)
+            rows = []
             for u in range(2):
                 part = total[:, 128 * u : 128 * u + 128]
                 halo = pltpu.roll(ze[...], 126 - 4 * (r + u), 1)
@@ -722,19 +734,22 @@
                     lane80 == LANES - 1, halo, pltpu.roll(part[160:240], LANES - 1, 1)
                 )
                 update = left + part[80:160] + right
-                new = xr[s, r + u + 2].astype(F32) + wet[r + u : r + u + 1] * update
-                finish_row(s, r + u, new)
-                if s + 1 < STEPS:
+                rows.append(xr[s, r + u + 2].astype(F32) + wet[r + u : r + u + 1] * update)
+            rows = finish_rows(s, r, rows)
+            if s + 1 < STEPS:
+                for u in range(2):
                     t = r + u + 2
+                    fill(t, rows[u])
                     eg[s + 1] = jnp.where(
-                        (lane80 >> 2) == t, pltpu.roll(new.astype(BF), 4 * t + 2, 1), eg[s + 1]
+                        (lane80 >> 2) == t, pltpu.roll(rows[u], 4 * t + 2, 1), eg[s + 1]
                     )
-            return c
-
-        run((0, 7), second_conv)
+
         if s + 1 < STEPS:
+            run((0, 7), second_conv)
             start_all(functools.partial(x_copy, s + 1), [(-1, 0), (1, 0)])
         run(range(1, 7), second_conv)
+        if s + 1 == STEPS:
+            run((0, 7), second_conv)
         if s + 1 < STEPS:
             corner_rows(s + 1)
             start_all(
@@ -746,7 +761,6 @@
             surface(s)
             s_all(start_all, s, True)
 
-        s_all(wait_arrivals, s, False)
         sources(s)
 
         @pl.when(ocean)
@@ -757,7 +771,7 @@
         def _(s=s):
             air_step(s)
 
-    out_ref[0] = flip[...].reshape(CH, ROWS, LANES).astype(BF)
+    out_ref[0] = jnp.transpose(final[...], (1, 0, 2))
 
     for s in range(STEPS):
         s_all(wait_departures, s, True)
@@ -797,7 +811,8 @@
                 pltpu.VMEM((9, 84, HO), BF),
                 pltpu.VMEM((HO,), F32),
                 pltpu.VMEM((9, CH, HO), BF),
-                pltpu.VMEM((CH * ROWS, LANES), F32),
+                pltpu.VMEM((LANES, LANES), F32),
+                pltpu.VMEM((ROWS, CH, LANES), BF),
                 pltpu.VMEM((STEPS, TALL, CH, LANES), BF),
                 pltpu.VMEM((STEPS, CH, LANES), BF),
                 pltpu.VMEM((STEPS, 2, CH, LANES), BF),
@@ -814,6 +829,7 @@
                 pltpu.VMEM((25, 2, 8, LANES), I32),
                 pltpu.VMEM((25, 2, 8, LANES), F32),
                 pltpu.VMEM((5, 10, 8, LANES), F32),
+                pltpu.VMEM((16, 2, 8, LANES), F32),
                 pltpu.VMEM((25, 8, LANES), F32),
                 pltpu.VMEM((24, 8, LANES), F32),
                 pltpu.VMEM((TALL, 256, LANES), BF),

time: 27 us -> 26.8 us (level)
  Pallas kernels: 25.2 us -> 24.9 us
where the time goes in v4:
time: 26.8 us; the launch traced here: 26.7 us
  Pallas kernels  24.9 us (93%)
  local copies, waits for them, and re-layouts  1.72 us (6%)
    pallas_call x1, Pallas kernels, local(): pl.pallas_call(functools.partial(kernel, lats, lons), out_shape=jax.Shape...  24.9 us
    unnamed x1, local copies, waits for them, and re-layouts  1.72 us

profile of v4, /device:TPU:102, one launch (start us, length us, event | category | flops | bytes accessed | tf_op | source)
XLA Modules:
  0.0 26.7 jit_solution(15729396053325654390)
XLA Ops:
  0.0 24.9 %shard_map.109 = bf16[1,80,16,128]{3,2,1,0:T(8,128)(2,1)} custom-call(bf16[1,80,16,128]{3,2,1,0:T(8,128)(2,1)} %state_hbm.1, s32[16,128]{1,0:T(8,128)} %mask_hbm.1, s32[1,2,4,16,128]{4,3,2,1,0:T(8,128)} %offsets_hbm.1, f32[1,4,16,128]{3,2,1,0:T(8,128)} %weights_hbm.1, f32[2,4,80]{2,1,0:T(4,128)} %proj_hbm.1, bf16[84,384]{1,0:T(8,128)(2,1)} %bitcast.5, ...), custom_call_target="tpu_custom_call" | custom-call | tf_op jit(solution)/shard_map/pallas_call | solution.py:797
  24.9 1.7 %copy.13 = bf16[1,80,16,128]{3,2,1,0:T(8,128)(2,1)} copy(bf16[1,80,16,128]{3,2,1,0:T(8,128)(2,1)} %shard_map.109) | data formatting | bytes 655360

commit v5 on v4

--- a/solution.py
+++ b/solution.py
@@ -246,6 +246,8 @@
 
     around = [(di, dj) for di in (-1, 1, 0) for dj in (-1, 1, 0)]
     ring = [(di, dj) for di, dj in around if di or dj]
+    beside_pairs = [(0, -1), (0, 1)]
+    corner_pairs = [(di, dj) for di, dj in ring if di and dj]
 
     def s_all(action, s, sending):
         @pl.when(air)
@@ -369,9 +371,6 @@
 
     @pl.when(ocean)
     def _():
-        edge_rows(0)
-        corner_rows(0)
-        eg[1] = jnp.zeros((CH, LANES), BF)
 
         def add(t, acc):
             return jnp.where((lane8 >> 2) == t, pltpu.roll(q[t], 4 * t + 2, 1), acc)
@@ -384,12 +383,20 @@
     neighbours = 1 + has[-1].astype(I32) + has[1].astype(I32)
     pl.semaphore_wait(barrier, 3 * neighbours + g * (3 * neighbours - 1))
 
+    @pl.when(ocean)
+    def _():
+        start_all(q_copy, ring)
+
     s_all(start_all, 0, True)
 
     @pl.when(ocean)
     def _():
-        start_all(q_copy, ring)
-        start_all(functools.partial(x_copy, 0), ring)
+        start_all(functools.partial(x_copy, 0), [(-1, 0), (1, 0)])
+        edge_rows(0)
+        start_all(functools.partial(x_copy, 0), beside_pairs)
+        corner_rows(0)
+        start_all(functools.partial(x_copy, 0), corner_pairs)
+        eg[1] = jnp.zeros((CH, LANES), BF)
         for t in range(2, 18):
             fill(t, xr[0, t])
 
@@ -672,52 +679,30 @@
             hid[h] = active[:, 0:128]
             hid[h + 1] = active[:, 128:256]
 
-        wait_arrivals(functools.partial(x_copy, s), [(0, -1), (0, 1)])
-        beside = jnp.where(pos < 2, eg_recv[s, 0], eg_recv[s, 1])
-        hh[...] = swapped(beside, pos)
-        for t in range(2, 18):
-            rim(t)
-        run(range(1, 8), first_conv)
-
-        wait_arrivals(functools.partial(x_copy, s), [(di, dj) for di, dj in ring if di])
-        own = eg[s]
-        for t in (0, 1, 18, 19):
-            own = jnp.where((lane80 >> 2) == t, pltpu.roll(xr[s, t], 4 * t + 2, 1), own)
-        ends = [jnp.where(pos16 < 2, cp_recv[s, n, 0], cp_recv[s, n, 1]) for n in range(2)]
-        corner = jnp.where(lane16 < 64, ends[0], ends[1])
-        corner = jnp.concatenate(
-            [pltpu.roll(corner, LANES - 8 * part, 1) if part else corner for part in range(5)], 0
-        )
-        beside = jnp.where((lane80 >= 8) & (lane80 < 72), beside, corner)
-        state_taps = taps(beside, own, pos)
-        for b in range(3):
-            x3e[CH * b : CH * b + CH] = state_taps[b]
-        hh[...] = swapped(beside, pos)
-        for t in (0, 1, 18, 19):
-            fill(t, xr[s, t])
-            rim(t)
-        run((0, 8), first_conv)
-
-        total = jnp.zeros((HOP, LANES), F32)
-        for a in range(3):
-            columns = x3e[...]
-            if a:
-                columns = pltpu.roll(columns, LANES - 4 * a, 1)
-            total = total + jnp.dot(w1[a], columns, preferred_element_type=F32)
-        slot = iota((HOP, LANES), 1) >> 2
-        outside = ((slot == 0) & (i == 0)) | ((slot == 17) & (i == lats - 1))
-        he[...] = jnp.where(outside, 0.0, gelu_of_twice(total)).astype(BF)
-        total = jnp.zeros((240, LANES), F32)
-        for a in range(3):
-            columns = he[...]
-            if a:
-                columns = pltpu.roll(columns, LANES - 4 * a, 1)
-            total = total + jnp.dot(w2[a], columns, preferred_element_type=F32)
-        ze[...] = jnp.where(
-            pos == 1,
-            pltpu.roll(total[160:240], LANES - 1, 1),
-            pltpu.roll(total[0:80], 1, 1),
-        )
+        def edge_tile(halo, mine):
+            state_taps = taps(halo, mine, pos)
+            for b in range(3):
+                x3e[CH * b : CH * b + CH] = state_taps[b]
+            total = jnp.zeros((HOP, LANES), F32)
+            for a in range(3):
+                columns = x3e[...]
+                if a:
+                    columns = pltpu.roll(columns, LANES - 4 * a, 1)
+                total = total + jnp.dot(w1[a], columns, preferred_element_type=F32)
+            slot = iota((HOP, LANES), 1) >> 2
+            outside = ((slot == 0) & (i == 0)) | ((slot == 17) & (i == lats - 1))
+            he[...] = jnp.where(outside, 0.0, gelu_of_twice(total)).astype(BF)
+            total = jnp.zeros((240, LANES), F32)
+            for a in range(3):
+                columns = he[...]
+                if a:
+                    columns = pltpu.roll(columns, LANES - 4 * a, 1)
+                total = total + jnp.dot(w2[a], columns, preferred_element_type=F32)
+            ze[...] = jnp.where(
+                pos == 1,
+                pltpu.roll(total[160:240], LANES - 1, 1),
+                pltpu.roll(total[0:80], 1, 1),
+            )
 
         def second_conv(p, c):
             r = 2 * p
@@ -744,17 +729,40 @@
                         (lane80 >> 2) == t, pltpu.roll(rows[u], 4 * t + 2, 1), eg[s + 1]
                     )
 
+        wait_arrivals(functools.partial(x_copy, s), [(0, -1), (0, 1)])
+        beside = jnp.where(pos < 2, eg_recv[s, 0], eg_recv[s, 1])
+        hh[...] = swapped(beside, pos)
+        for t in range(2, 18):
+            rim(t)
+        run(range(1, 8), first_conv)
+        if s + 1 == STEPS:
+            edge_tile(beside, eg[s])
+            run(range(1, 7), second_conv)
+
+        wait_arrivals(functools.partial(x_copy, s), [(di, dj) for di, dj in ring if di])
+        own = eg[s]
+        for t in (0, 1, 18, 19):
+            own = jnp.where((lane80 >> 2) == t, pltpu.roll(xr[s, t], 4 * t + 2, 1), own)
+        ends = [jnp.where(pos16 < 2, cp_recv[s, n, 0], cp_recv[s, n, 1]) for n in range(2)]
+        corner = jnp.where(lane16 < 64, ends[0], ends[1])
+        corner = jnp.concatenate(
+            [pltpu.roll(corner, LANES - 8 * part, 1) if part else corner for part in range(5)], 0
+        )
+        beside = jnp.where((lane80 >= 8) & (lane80 < 72), beside, corner)
+        hh[...] = swapped(beside, pos)
+        for t in (0, 1, 18, 19):
+            fill(t, xr[s, t])
+            rim(t)
+        run((0, 8), first_conv)
+        edge_tile(beside, own)
+        run((0, 7), second_conv)
+
         if s + 1 < STEPS:
-            run((0, 7), second_conv)
             start_all(functools.partial(x_copy, s + 1), [(-1, 0), (1, 0)])
-        run(range(1, 7), second_conv)
-        if s + 1 == STEPS:
-            run((0, 7), second_conv)
-        if s + 1 < STEPS:
+            run(range(1, 7), second_conv)
+            start_all(functools.partial(x_copy, s + 1), beside_pairs)
             corner_rows(s + 1)
-            start_all(
-                functools.partial(x_copy, s + 1), [(di, dj) for di, dj in ring if dj]
-            )
+            start_all(functools.partial(x_copy, s + 1), corner_pairs)
 
     for s in range(STEPS):
         if s:

time: 26.8 us -> 26.5 us (0.989)
  no operation moved by 1% of the time
where the time goes in v5:
time: 26.5 us; the launch traced here: 26.4 us
  Pallas kernels  24.7 us (93%)
  local copies, waits for them, and re-layouts  1.72 us (6%)
    pallas_call x1, Pallas kernels, local(): pl.pallas_call(functools.partial(kernel, lats, lons), out_shape=jax.Shape...  24.7 us
    unnamed x1, local copies, waits for them, and re-layouts  1.72 us

profile of v5, /device:TPU:102, one launch (start us, length us, event | category | flops | bytes accessed | tf_op | source)
XLA Modules:
  0.0 26.4 jit_solution(1370489840783223919)
XLA Ops:
  0.0 24.7 %shard_map.109 = bf16[1,80,16,128]{3,2,1,0:T(8,128)(2,1)} custom-call(bf16[1,80,16,128]{3,2,1,0:T(8,128)(2,1)} %state_hbm.1, s32[16,128]{1,0:T(8,128)} %mask_hbm.1, s32[1,2,4,16,128]{4,3,2,1,0:T(8,128)} %offsets_hbm.1, f32[1,4,16,128]{3,2,1,0:T(8,128)} %weights_hbm.1, f32[2,4,80]{2,1,0:T(4,128)} %proj_hbm.1, bf16[84,384]{1,0:T(8,128)(2,1)} %bitcast.5, ...), custom_call_target="tpu_custom_call" | custom-call | tf_op jit(solution)/shard_map/pallas_call | solution.py:805
  24.7 1.7 %copy.13 = bf16[1,80,16,128]{3,2,1,0:T(8,128)(2,1)} copy(bf16[1,80,16,128]{3,2,1,0:T(8,128)(2,1)} %shard_map.109) | data formatting | bytes 655360

commit v6 on v5

--- a/solution.py
+++ b/solution.py
@@ -819,7 +819,7 @@
                 pltpu.VMEM((9, 84, HO), BF),
                 pltpu.VMEM((HO,), F32),
                 pltpu.VMEM((9, CH, HO), BF),
-                pltpu.VMEM((LANES, LANES), F32),
+                pltpu.VMEM((2 * LANES, LANES), F32),
                 pltpu.VMEM((ROWS, CH, LANES), BF),
                 pltpu.VMEM((STEPS, TALL, CH, LANES), BF),
                 pltpu.VMEM((STEPS, CH, LANES), BF),

time: 26.5 us -> 26.5 us (level)
  no operation moved by 1% of the time
where the time goes in v6:
time: 26.5 us; the launch traced here: 26.4 us
  Pallas kernels  24.7 us (93%)
  local copies, waits for them, and re-layouts  1.72 us (6%)
    pallas_call x1, Pallas kernels, local(): pl.pallas_call(functools.partial(kernel, lats, lons), out_shape=jax.Shape...  24.7 us
    unnamed x1, local copies, waits for them, and re-layouts  1.72 us

profile of v6, /device:TPU:102, one launch (start us, length us, event | category | flops | bytes accessed | tf_op | source)
XLA Modules:
  0.0 26.4 jit_solution(13142616868466567385)
XLA Ops:
  0.0 24.7 %shard_map.109 = bf16[1,80,16,128]{3,2,1,0:T(8,128)(2,1)} custom-call(bf16[1,80,16,128]{3,2,1,0:T(8,128)(2,1)} %state_hbm.1, s32[16,128]{1,0:T(8,128)} %mask_hbm.1, s32[1,2,4,16,128]{4,3,2,1,0:T(8,128)} %offsets_hbm.1, f32[1,4,16,128]{3,2,1,0:T(8,128)} %weights_hbm.1, f32[2,4,80]{2,1,0:T(4,128)} %proj_hbm.1, bf16[84,384]{1,0:T(8,128)(2,1)} %bitcast.5, ...), custom_call_target="tpu_custom_call" | custom-call | tf_op jit(solution)/shard_map/pallas_call | solution.py:805
  24.7 1.7 %copy.13 = bf16[1,80,16,128]{3,2,1,0:T(8,128)(2,1)} copy(bf16[1,80,16,128]{3,2,1,0:T(8,128)(2,1)} %shard_map.109) | data formatting | bytes 655360
